TPU v7x, 128 devices: a whole 4x4x4 slice. The times are simulated.
128 devices in a mesh: dp: 16 (over x_hi, y, core), tensor: 8 (over x_lo, z).
Axes of the slice: x: 4 (x_hi: 2, x_lo: 2; x = x_hi * 2 + x_lo), y: 4, z: 4, core: 2. Of those that a mesh axis runs over, the one named last changes fastest.
Arguments:
- train_acts: bfloat16 [2048, 5120], P('dp', 'tensor'), may hold values from -6 to 6
- train_grads: bfloat16 [2048, 13824], P('dp', 'tensor'), may hold values from -0.0011672974 to 0.0011672974
- query_acts: bfloat16 [128, 5120], P('dp', 'tensor'), may hold values from -6 to 6
- query_grads: bfloat16 [128, 13824], P('dp', 'tensor'), may hold values from -6 to 6
- in_basis: bfloat16 [5120, 5120], P('dp', 'tensor'), may hold values from -0.078125 to 0.078125
- out_basis: bfloat16 [13824, 13824], P('tensor', 'dp'), may hold values from -0.0546875 to 0.0546875
- eigvals: float32 [13824, 5120], P('dp', 'tensor'), may hold values from 0.02 to 5
- lengths: int32 [16], P('dp'), may hold values from 32 to 128, as said below
Outputs:
- token_scores: float32 [2, 2048], P(None, ('dp', 'tensor'))
- seq_scores: float32 [2, 16], P(None, 'dp')
Inputs may be any that keep to these rules, and one draw needn't show every extreme that they name: `lengths`: each sequence's valid tokens come first and the rest is padding.
All inputs are finite; a program needn't handle non-finite values.
Results may differ from a plain program's by a relative error of at most 0.0053.
Values may be sent and summed in bfloat16 or wider, within the bound.
No kernel may reach another device: no remote copies, remote signals or barrier semaphores. Data moves between devices by JAX's collectives and lax.ppermute only.
A program may use at most 128 MiB of HBM per device.

v0:
```python
import jax
import jax.numpy as jnp
from jax import lax
from jax.sharding import PartitionSpec as P

SEQLEN = 128
QUERIES = 2


damping = 0.1


def per_device(
    train_acts, train_grads, query_acts, query_grads, in_basis, out_basis, eigvals, lengths
):
    tok_rows = train_acts.shape[0]
    query_rows = query_acts.shape[0]
    block_rows = tok_rows + query_rows
    n_data = lax.axis_size("dp")
    n_tensor = lax.axis_size("tensor")
    grad_local = jnp.concatenate([train_grads, query_grads], axis=0)
    grad_partial = jnp.dot(
        lax.all_gather(grad_local, "dp", axis=0, tiled=True),
        out_basis,
        preferred_element_type=jnp.float32,
    )
    rotated_grads = lax.psum(grad_partial, "tensor").astype(jnp.bfloat16)
    grouped_grads = rotated_grads.reshape(n_data, block_rows, rotated_grads.shape[1])
    train_rot_grads = grouped_grads[:, :tok_rows].reshape(n_data * tok_rows, -1)
    query_rot_grads = grouped_grads[:, tok_rows:].reshape(n_data * query_rows, -1)
    act_local = jnp.concatenate([train_acts, query_acts], axis=0)
    widened = lax.all_gather(act_local, "tensor", axis=1, tiled=True)
    blocks = lax.all_to_all(widened, "dp", split_axis=1, concat_axis=0, tiled=True)
    act_partial = jnp.dot(blocks, in_basis, preferred_element_type=jnp.float32)
    rotated_acts = lax.psum(act_partial, "dp").astype(jnp.bfloat16)
    grouped_acts = rotated_acts.reshape(n_data, block_rows, rotated_acts.shape[1])
    train_rot_acts = grouped_acts[:, :tok_rows].reshape(n_data * tok_rows, -1)
    query_rot_acts = grouped_acts[:, tok_rows:].reshape(n_data * query_rows, -1)
    query_len = query_rot_grads.shape[0] // QUERIES
    acts_wide = train_rot_acts.astype(jnp.float32)
    divisor = query_len * (eigvals + damping)
    results = []
    for query in range(QUERIES):
        grad_part = query_rot_grads[query * query_len : (query + 1) * query_len]
        act_part = query_rot_acts[query * query_len : (query + 1) * query_len]
        numerator = jnp.dot(grad_part.T, act_part, preferred_element_type=jnp.float32)
        precond = (numerator / divisor).astype(jnp.bfloat16)
        projected = jnp.dot(train_rot_grads, precond, preferred_element_type=jnp.float32)
        results.append(jnp.sum(projected * acts_wide, axis=1))
    partial_scores = jnp.stack(results, axis=0)
    seq_count = lengths.shape[0]
    own_count = tok_rows // n_tensor
    seq_ids = jnp.arange(seq_count, dtype=jnp.int32)
    shares = lax.psum_scatter(partial_scores, ("dp", "tensor"), scatter_dimension=1, tiled=True)
    offsets = lax.axis_index("tensor") * own_count + jnp.arange(own_count, dtype=jnp.int32)
    member = (offsets // SEQLEN)[:, None] == seq_ids[None, :]
    limits = jnp.sum(jnp.where(member, lengths[None, :], 0), axis=1)
    valid = (offsets % SEQLEN < limits).astype(jnp.float32)
    token_scores = shares * valid[None, :]
    seq_partial = jnp.sum(token_scores[:, :, None] * member.astype(jnp.float32)[None, :, :], axis=1)
    seq_scores = lax.psum(seq_partial, "tensor")
    return (token_scores, seq_scores)


def solution(mesh):
    placed = (
        P("dp", "tensor"),
        P("dp", "tensor"),
        P("dp", "tensor"),
        P("dp", "tensor"),
        P("dp", "tensor"),
        P("tensor", "dp"),
        P("dp", "tensor"),
        P("dp"),
    )
    return jax.shard_map(
        per_device,
        mesh=mesh,
        in_specs=placed,
        out_specs=(P(None, ("dp", "tensor")), P(None, "dp")),
        check_vma=False,
    )
```

profile of v0, /device:TPU:1, one launch (start us, length us, event | category | flops | bytes accessed | tf_op | source)
XLA Modules:
  0.0 1057.4 jit_solution(9556666658992773922)
XLA Ops:
  7.2 1.8 pad_maximum_fusion.1
  9.1 1.2 copy.16
  10.3 1.6 pad_maximum_fusion
  11.9 35.3 %all-gather.5.cloned.1.call-done = bf16[136,5120]{1,0:T(8,128)(2,1)} async-done(((bf16[136,640]{1,0:T(8,128)(2,1)}), bf16[136,5120]{1,0:T(8,128)(2,1)}) %all-gather.5.cloned.1.call-update) | async-done | bytes 1392656 | tf_op jit(solution)/shard_map/all_gather | solution.py:32
  47.2 4.0 all_to_all.14
  51.2 3.0 copy.18
  54.3 12.9 %all-to-all-start = ((bf16[136,16,320]{2,0,1:T(8,128)(2,1)}), bf16[136,16,320]{2,0,1:T(8,128)(2,1)}, u32[]{:S(2)}, u32[]{:S(2)}) async-start(bf16[136,16,320]{2,0,1:T(8,128)(2,1)} %copy.18), calls=%async_computation | async-start | bytes 3342336 | tf_op jit(solution)/shard_map/all_to_all | solution.py:33
  67.8 27.2 %all-to-all-done = bf16[136,16,320]{2,0,1:T(8,128)(2,1)} async-done(((bf16[136,16,320]{2,0,1:T(8,128)(2,1)}), bf16[136,16,320]{2,0,1:T(8,128)(2,1)}, u32[]{:S(2)}, u32[]{:S(2)}) %all-to-all-start) | async-done | bytes 1392672 | tf_op jit(solution)/shard_map/all_to_all | solution.py:33
  95.0 5.6 fusion.15
  100.7 107.4 %all-reduce.3 = bf16[2176,640]{1,0:T(8,128)(2,1)} all-reduce(f32[2176,640]{1,0:T(8,128)} %fusion.15), channel_id=1, replica_groups=mesh['dp'=16,'tensor'=8] {'dp'}, use_global_device_ids=true, to_apply=%region_1.0 | all-reduce | flops 1392640 | bytes 8355840 | tf_op jit(solution)/shard_map/psum | solution.py:35
  208.1 2.0 slice.37
  210.0 2.9 bitcast_convert_fusion
  212.9 5.9 copy.19
  218.8 12.5 %fusion.14 = f32[2176,864]{0,1:T(8,128)} fusion(bf16[2176,1728]{1,0:T(8,128)(2,1)} %all-gather.3.cloned.1.call-done, bf16[1728,864]{1,0:T(8,128)(2,1)S(1)} %copy-done), kind=kOutput, calls=%fused_computation.30 | convolution fusion | flops 6497501184 | bytes 18026496 | tf_op jit(solution)/shard_map/dot_general | solution.py:22
  231.3 144.8 %all-reduce.2 = bf16[2176,864]{0,1:T(8,128)(2,1)} all-reduce(f32[2176,864]{0,1:T(8,128)} %fusion.14), channel_id=1, replica_groups=mesh['dp'=16,'tensor'=8] {'tensor'}, use_global_device_ids=true, to_apply=%region_0.0 | all-reduce | flops 1880064 | bytes 11280384 | tf_op jit(solution)/shard_map/psum | solution.py:27
  376.1 6.3 copy.17
  382.3 4.3 slice.34
  386.6 7.7 multiply_reduce_fusion
  394.3 7.7 multiply_reduce_fusion.1
  402.0 1.4 copy.21
  403.4 632.5 %reduce-scatter.4.cloned.1.call-done = f32[16,2]{1,0:T(8,128)} async-done(((f32[2048,2]{1,0:T(8,128)}), f32[16,2]{1,0:T(8,128)}) %reduce-scatter.4.cloned.1.call-update) | async-done | bytes 144
  1036.0 0.8 copy.22
  1036.7 0.7 multiply_reduce_fusion.2
  1037.4 13.5 %psum.23 = f32[2,1]{0,1:T(1,128)} all-reduce(f32[2,1]{0,1:T(1,128)S(1)} %bitcast.46), channel_id=1, replica_groups=mesh['dp'=16,'tensor'=8] {'tensor'}, use_global_device_ids=true, to_apply=%region_6.7 | all-reduce | flops 2 | bytes 16 | tf_op jit(solution)/shard_map/psum | solution.py:61
  (13 shorter events, 0.2 us)
Async XLA Ops:
  7.2 211.7 %copy-start = (bf16[1728,864]{1,0:T(8,128)(2,1)S(1)}, bf16[1728,864]{1,0:T(8,128)(2,1)}, u32[]{:S(2)}) copy-start(bf16[1728,864]{1,0:T(8,128)(2,1)} %param.13) | copy-start | bytes 8957956
  7.2 40.0 %all-gather.5.cloned.1.call-start = ((), (), s32[]{:S(2)}) async-start(), calls=%async_computation.3 | async-start | bytes 1566720 | tf_op jit(solution)/shard_map/all_gather | solution.py:32
  9.0 209.8 %all-gather.3.cloned.1.call-start = ((), (), s32[]{:S(2)}) async-start(), calls=%async_computation.2 | async-start | bytes 8286208 | tf_op jit(solution)/shard_map/all_gather | solution.py:23
  51.2 43.8 %copy-start.1 = (bf16[320,640]{1,0:T(8,128)(2,1)S(1)}, bf16[320,640]{1,0:T(8,128)(2,1)}, u32[]{:S(2)}) copy-start(bf16[320,640]{1,0:T(8,128)(2,1)} %param.12) | copy-start | bytes 1228804
  54.3 40.8 %all-to-all-start = ((bf16[136,16,320]{2,0,1:T(8,128)(2,1)}), bf16[136,16,320]{2,0,1:T(8,128)(2,1)}, u32[]{:S(2)}, u32[]{:S(2)}) async-start(bf16[136,16,320]{2,0,1:T(8,128)(2,1)} %copy.18), calls=%async_computation | async-start | bytes 3342336 | tf_op jit(solution)/shard_map/all_to_all | solution.py:33
  67.1 968.8 %reduce-scatter.4.cloned.1.call-start = ((), (), s32[]{:S(2)}) async-start(), calls=%async_computation.4 | async-start | bytes 1056768
Sparse Core Ops, SparseCore 0:
  9.7 37.4 all-gather.4
  49.6 112.4 all-gather.2
  403.5 632.3 reduce-scatter.3
where the time goes:
time: 1080 us; the launch traced here: 1060 us
  waiting for transfers between devices  695 us (64%)
  blocking collectives  266 us (25%)
  matrix products  33.5 us (3%)
  local copies, waits for them, and re-layouts  28.9 us (3%)
  between operations  14.5 us (1%)
  starting transfers between devices  13 us (1%)
    unnamed x4, waiting for transfers between devices  633 us
    psum x1, blocking collectives, per_device(): rotated_grads = lax.psum(grad_partial, 'tensor').astype(jnp.bfloat16)  145 us
    psum x1, blocking collectives, per_device(): rotated_acts = lax.psum(act_partial, 'dp').astype(jnp.bfloat16)  107 us
    all_gather x1, waiting for transfers between devices, per_device(): widened = lax.all_gather(act_local, 'tensor', axis=1, tiled=True)  35.3 us
    all_to_all x1, waiting for transfers between devices, per_device(): lax.all_to_all(widened, 'dp', split_axis=1, concat_axis=0, tiled=True)  27.2 us
  transfers between devices with their start and end apart: 4, of which 3 were waited for; matrix products, arithmetic and copies ran while one was open for 2% of the time, Pallas kernels for 0%

commit v1 on v0

--- a/solution.py
+++ b/solution.py
@@ -48,17 +48,19 @@
         projected = jnp.dot(train_rot_grads, precond, preferred_element_type=jnp.float32)
         results.append(jnp.sum(projected * acts_wide, axis=1))
     partial_scores = jnp.stack(results, axis=0)
-    seq_count = lengths.shape[0]
     own_count = tok_rows // n_tensor
-    seq_ids = jnp.arange(seq_count, dtype=jnp.int32)
-    shares = lax.psum_scatter(partial_scores, ("dp", "tensor"), scatter_dimension=1, tiled=True)
-    offsets = lax.axis_index("tensor") * own_count + jnp.arange(own_count, dtype=jnp.int32)
-    member = (offsets // SEQLEN)[:, None] == seq_ids[None, :]
-    limits = jnp.sum(jnp.where(member, lengths[None, :], 0), axis=1)
-    valid = (offsets % SEQLEN < limits).astype(jnp.float32)
-    token_scores = shares * valid[None, :]
-    seq_partial = jnp.sum(token_scores[:, :, None] * member.astype(jnp.float32)[None, :, :], axis=1)
-    seq_scores = lax.psum(seq_partial, "tensor")
+    by_sequence = partial_scores.reshape(QUERIES, n_data, tok_rows).transpose(1, 0, 2)
+    spread = jnp.broadcast_to(by_sequence[:, None], (n_data, n_tensor, QUERIES, tok_rows))
+    received = lax.all_to_all(
+        spread.reshape(n_data * n_tensor, QUERIES, tok_rows), ("dp", "tensor"), 0, 0, tiled=True
+    )
+    raw = jnp.sum(received, axis=0)
+    valid = (jnp.arange(tok_rows, dtype=jnp.int32) % SEQLEN < lengths[0]).astype(jnp.float32)
+    scores = raw * valid[None, :]
+    seq_scores = jnp.sum(scores, axis=1, keepdims=True)
+    token_scores = lax.dynamic_slice_in_dim(
+        scores, lax.axis_index("tensor") * own_count, own_count, axis=1
+    )
     return (token_scores, seq_scores)
 
 

time: 1080 us -> 436 us (0.40); the launches traced: 1060 us -> 435 us
  waiting for transfers between devices: 695 us -> 44.6 us
  blocking collectives: 266 us -> 292 us
    unnamed x4 -> x2, waiting for transfers between devices: 633 us -> 0.03 us
    all_to_all x0 -> x1, blocking collectives: none -> 41.3 us  [per_device(): lax.all_to_all(widened, 'dp', split_axis=1, concat_axis=0, tiled=True)]
    all_to_all x1, waiting for transfers between devices: 27.2 us -> 9.28 us  [per_device(): lax.all_to_all(spread.reshape(n_data * n_tensor, QUERIES, tok_rows), ('dp...]
    psum x1 -> x0, blocking collectives: 13.5 us -> none  [per_device(): seq_scores = lax.psum(seq_partial, 'tensor')]
  transfers between devices with their start and end apart: 4 -> 3, of which waited for: 3 -> 2; matrix products, arithmetic and copies ran while one was open for 2% -> 5% of each run, Pallas kernels for 0% -> 0%
where the time goes in v1:
time: 436 us; the launch traced here: 435 us
  blocking collectives  292 us (67%)
  waiting for transfers between devices  44.6 us (10%)
  matrix products  32.1 us (7%)
  local copies, waits for them, and re-layouts  26.8 us (6%)
  starting transfers between devices  17.9 us (4%)
  between operations  14.8 us (3%)
  other arithmetic  6.99 us (2%)
    psum x1, blocking collectives, per_device(): rotated_grads = lax.psum(grad_partial, 'tensor').astype(jnp.bfloat16)  145 us
    psum x1, blocking collectives, per_device(): rotated_acts = lax.psum(act_partial, 'dp').astype(jnp.bfloat16)  106 us
    all_to_all x1, blocking collectives, per_device(): lax.all_to_all(widened, 'dp', split_axis=1, concat_axis=0, tiled=True)  41.3 us
    all_gather x1, waiting for transfers between devices, per_device(): widened = lax.all_gather(act_local, 'tensor', axis=1, tiled=True)  35.3 us
    all_to_all x1, starting transfers between devices, per_device(): lax.all_to_all(spread.reshape(n_data * n_tensor, QUERIES, tok_rows), ('dp...  17.8 us
    dot_general x2, matrix products, per_device(): jnp.dot(train_rot_grads, precond, preferred_element_type=jnp.float32)  15.4 us
    dot_general x1, matrix products, per_device(): jnp.dot(lax.all_gather(grad_local, 'dp', axis=0, tiled=True), out_basis,...  12.5 us
    all_to_all x1, waiting for transfers between devices, per_device(): lax.all_to_all(spread.reshape(n_data * n_tensor, QUERIES, tok_rows), ('dp...  9.28 us
  transfers between devices with their start and end apart: 3, of which 2 were waited for; matrix products, arithmetic and copies ran while one was open for 5% of the time, Pallas kernels for 0%

profile of v1, /device:TPU:1, one launch (start us, length us, event | category | flops | bytes accessed | tf_op | source)
XLA Modules:
  0.0 435.2 jit_solution(11287337305493497635)
XLA Ops:
  7.2 1.8 pad_maximum_fusion.1
  9.1 1.2 copy.29
  10.3 1.6 pad_maximum_fusion
  11.9 35.3 %all-gather.5.cloned.1.call-done = bf16[136,5120]{1,0:T(8,128)(2,1)} async-done(((bf16[136,640]{1,0:T(8,128)(2,1)}), bf16[136,5120]{1,0:T(8,128)(2,1)}) %all-gather.5.cloned.1.call-update) | async-done | bytes 1392656 | tf_op jit(solution)/shard_map/all_gather | solution.py:32
  47.2 4.0 all_to_all.17
  51.2 1.9 copy.31
  53.1 41.3 %all_to_all.24 = bf16[136,16,320]{2,0,1:T(8,128)(2,1)S(1)} all-to-all(bf16[136,16,320]{2,0,1:T(8,128)(2,1)S(1)} %copy.31), channel_id=1, replica_groups=mesh['dp'=16,'tensor'=8] {'dp'}, dimensions={1} | all-to-all | bytes 2785280 | tf_op jit(solution)/shard_map/all_to_all | solution.py:33
  94.4 4.2 fusion.16
  98.6 106.1 %all-reduce.3 = bf16[2176,640]{1,0:T(8,128)(2,1)} all-reduce(f32[2176,640]{1,0:T(8,128)} %fusion.16), channel_id=1, replica_groups=mesh['dp'=16,'tensor'=8] {'dp'}, use_global_device_ids=true, to_apply=%region_1.0 | all-reduce | flops 1392640 | bytes 8355840 | tf_op jit(solution)/shard_map/psum | solution.py:35
  204.7 2.0 slice.37
  206.7 2.9 bitcast_convert_fusion
  209.5 5.9 %copy.32 = f32[2048,640]{0,1:T(8,128)} copy(f32[2048,640]{1,0:T(8,128)} %bitcast_convert_fusion) | data formatting | bytes 10485760 | tf_op jit(solution)/shard_map/convert_element_type | solution.py:40
  215.5 12.5 %fusion.15 = f32[2176,864]{0,1:T(8,128)} fusion(bf16[2176,1728]{1,0:T(8,128)(2,1)} %all-gather.3.cloned.1.call-done, bf16[1728,864]{1,0:T(8,128)(2,1)S(1)} %copy-done), kind=kOutput, calls=%fused_computation.24 | convolution fusion | flops 6497501184 | bytes 18026496 | tf_op jit(solution)/shard_map/dot_general | solution.py:22
  228.0 144.6 %all-reduce.2 = bf16[2176,864]{0,1:T(8,128)(2,1)} all-reduce(f32[2176,864]{0,1:T(8,128)} %fusion.15), channel_id=1, replica_groups=mesh['dp'=16,'tensor'=8] {'tensor'}, use_global_device_ids=true, to_apply=%region_0.0 | all-reduce | flops 1880064 | bytes 11280384 | tf_op jit(solution)/shard_map/psum | solution.py:27
  372.5 6.3 %copy.30 = bf16[2176,864]{1,0:T(8,128)(2,1)} copy(bf16[2176,864]{0,1:T(8,128)(2,1)} %all-reduce.2) | data formatting | bytes 7520256 | tf_op jit(solution)/shard_map/convert_element_type | solution.py:27
  378.8 4.3 slice.34
  383.1 7.7 %multiply_reduce_fusion = f32[2048]{0:T(1024)S(1)} fusion(f32[2048,640]{0,1:T(8,128)} %copy.32, bf16[2048,864]{1,0:T(8,128)(2,1)} %bitcast.42, f32[864,640]{1,0:T(8,128)} %param.14, bf16[16,136,864]{2,1,0:T(8,128)(2,1)} %bitcast.36, bf16[16,136,640]{2,1,0:T(8,128)(2,1)} %bitcast.39), kind=kOutput, calls=%fused_computation | convolution fusion | flops 2340534272 | bytes 11329536 | tf_op jit(solution)/shard_map/dot_general | solution.py:48
  390.8 7.7 %multiply_reduce_fusion.1 = f32[2048]{0:T(1024)S(1)} fusion(f32[2048,640]{0,1:T(8,128)} %copy.32, bf16[2048,864]{1,0:T(8,128)(2,1)} %bitcast.43, f32[864,640]{1,0:T(8,128)} %param.14, bf16[16,136,864]{2,1,0:T(8,128)(2,1)} %bitcast.37, bf16[16,136,640]{2,1,0:T(8,128)(2,1)} %bitcast.40), kind=kOutput, calls=%fused_computation.1 | convolution fusion | flops 2340534272 | bytes 11329536 | tf_op jit(solution)/shard_map/dot_general | solution.py:48
  398.5 0.7 broadcast_in_dim.4
  399.1 17.8 %all-to-all-start.1 = ((f32[128,2,128]{2,1,0:T(2,128)}), f32[128,2,128]{2,1,0:T(2,128)S(1)}, u32[]{:S(2)}, u32[]{:S(2)}) async-start(f32[128,2,128]{2,1,0:T(2,128)} %bitcast.12), calls=%async_computation.1 | async-start | bytes 262144 | tf_op jit(solution)/shard_map/all_to_all | solution.py:54
  417.6 9.3 %all-to-all-done.1 = f32[128,2,128]{2,1,0:T(2,128)S(1)} async-done(((f32[128,2,128]{2,1,0:T(2,128)}), f32[128,2,128]{2,1,0:T(2,128)S(1)}, u32[]{:S(2)}, u32[]{:S(2)}) %all-to-all-start.1) | async-done | bytes 131104 | tf_op jit(solution)/shard_map/all_to_all | solution.py:54
  426.9 0.1 reduce_sum.38
  427.1 0.6 fusion.14
  427.7 0.6 constant_dynamic-slice_fusion
  (11 shorter events, 0.2 us)
Async XLA Ops:
  7.2 208.3 %copy-start = (bf16[1728,864]{1,0:T(8,128)(2,1)S(1)}, bf16[1728,864]{1,0:T(8,128)(2,1)}, u32[]{:S(2)}) copy-start(bf16[1728,864]{1,0:T(8,128)(2,1)} %param.13) | copy-start | bytes 8957956
  7.2 40.0 %all-gather.5.cloned.1.call-start = ((), (), s32[]{:S(2)}) async-start(), calls=%async_computation.3 | async-start | bytes 1566720 | tf_op jit(solution)/shard_map/all_gather | solution.py:32
  9.0 206.5 %all-gather.3.cloned.1.call-start = ((), (), s32[]{:S(2)}) async-start(), calls=%async_computation.2 | async-start | bytes 8286208 | tf_op jit(solution)/shard_map/all_gather | solution.py:23
  51.2 43.1 %copy-start.1 = (bf16[320,640]{1,0:T(8,128)(2,1)S(1)}, bf16[320,640]{1,0:T(8,128)(2,1)}, u32[]{:S(2)}) copy-start(bf16[320,640]{1,0:T(8,128)(2,1)} %param.12) | copy-start | bytes 1228804
  399.1 27.8 %all-to-all-start.1 = ((f32[128,2,128]{2,1,0:T(2,128)}), f32[128,2,128]{2,1,0:T(2,128)S(1)}, u32[]{:S(2)}, u32[]{:S(2)}) async-start(f32[128,2,128]{2,1,0:T(2,128)} %bitcast.12), calls=%async_computation.1 | async-start | bytes 262144 | tf_op jit(solution)/shard_map/all_to_all | solution.py:54
Sparse Core Ops, SparseCore 0:
  9.7 37.4 all-gather.4
  49.6 107.6 all-gather.2

commit v2 on v1

v2 whole, which is shorter than its diff:
```python
import jax
import jax.numpy as jnp
from jax import lax
from jax.experimental import pallas as pl
from jax.experimental.pallas import tpu as pltpu
from jax.sharding import PartitionSpec as P

SEQLEN = 128
QUERIES = 2
AXES = ("x_hi", "y", "core", "x_lo", "z")
CHIPS = ("x_hi", "y")
TENSOR = ("x_lo", "z")
SIZES = (2, 4, 2, 2, 4)
ROWS = 16
LANES = 128
GROUP = 4
VMEM_BYTES = 24 * 1024 * 1024
VMEM = pl.BlockSpec(memory_space=pltpu.VMEM)
SMEM = pl.BlockSpec(memory_space=pltpu.SMEM)
PARAMS = pltpu.CompilerParams(vmem_limit_bytes=VMEM_BYTES)


damping = 0.1


def take(x, axis, step):
    count = lax.axis_size(axis)
    return lax.ppermute(x, axis, [(i, (i - step) % count) for i in range(count)])


def after(x, *earlier):
    return lax.optimization_barrier((x,) + earlier)[0]


def turn(blocks, axis, shift):
    count = blocks.shape[axis]
    return lax.dynamic_slice_in_dim(
        jnp.concatenate([blocks, blocks], axis=axis), shift, count, axis=axis
    )


def pick_kernel(order, blocks, out):
    for i in range(out.shape[0]):
        out[i] = blocks[order[i]]


def pick(order, blocks):
    return pl.pallas_call(
        pick_kernel,
        out_shape=jax.ShapeDtypeStruct(blocks.shape, blocks.dtype),
        in_specs=[SMEM, VMEM],
        out_specs=VMEM,
        compiler_params=PARAMS,
        name="pick",
    )(order, blocks)


def own_rows_first(rows, x_lo, z):
    order = jnp.stack([(x_lo ^ dx) * 4 + (z + dz) % 4 for dz in range(4) for dx in range(2)])
    return pick(order.astype(jnp.int32), rows.reshape(8, ROWS, -1)).reshape(rows.shape)


def both_cores(x):
    x = x.astype(jnp.float32)
    other = take(x, "core", 1)
    one, two = lax.optimization_barrier(
        (jnp.concatenate([x, other], axis=0), jnp.concatenate([other, x], axis=0))
    )
    return one.astype(jnp.bfloat16), two.astype(jnp.bfloat16)


def rotate_kernel(g0, g1, g2, g3, own_basis, sib_basis, near, up, down, far_own, far_sib, query):
    rows = jnp.concatenate([g0[...], g1[...], g2[...], g3[...]], axis=0)
    shard = g0.shape[0]
    for block, basis in enumerate((own_basis, sib_basis)):
        product = jnp.dot(rows, basis[...], preferred_element_type=jnp.float32)
        for dz in range(4):
            for dx in range(2):
                for s in range(GROUP):
                    start = s * shard + (dz * 2 + dx) * ROWS
                    piece = product[start : start + ROWS]
                    at = (dx * GROUP + s) * ROWS
                    if dz == 2:
                        target = (far_own, far_sib)[block]
                        target[at : at + ROWS, :] = piece
                    else:
                        target = (near, up, None, down)[dz]
                        target[block, at : at + ROWS, :] = piece
        if block == 0:
            for s in range(GROUP):
                start = s * shard + SEQLEN
                query[s] = product[start : start + ROWS]


def rotate(shards, own_basis, sib_basis):
    width = own_basis.shape[1]
    pair = jax.ShapeDtypeStruct((2, 2 * GROUP * ROWS, width), jnp.float32)
    single = jax.ShapeDtypeStruct((2 * GROUP * ROWS, width), jnp.float32)
    query = jax.ShapeDtypeStruct((GROUP, ROWS, width), jnp.float32)
    return pl.pallas_call(
        rotate_kernel,
        out_shape=(pair, pair, pair, single, single, query),
        in_specs=[VMEM] * 6,
        out_specs=(VMEM,) * 6,
        compiler_params=PARAMS,
        cost_estimate=pl.CostEstimate(
            flops=2 * 576 * 1728 * 1728, bytes_accessed=12 * 1024 * 1024, transcendentals=0
        ),
        name="rotate",
    )(*shards, own_basis, sib_basis)


def sum_z_kernel(near, up, down, kept, other):
    half = GROUP * ROWS
    for block in range(2):
        total = near[block] + up[block] + down[block]
        kept[block] = total[:half]
        other[block] = total[half:]


def sum_z(*arrays):
    width = arrays[0].shape[2]
    part = jax.ShapeDtypeStruct((2, GROUP * ROWS, width), jnp.float32)
    return pl.pallas_call(
        sum_z_kernel,
        out_shape=(part, part),
        in_specs=[VMEM] * 3,
        out_specs=(VMEM, VMEM),
        compiler_params=PARAMS,
        cost_estimate=pl.CostEstimate(
            flops=4 * 64 * 864, bytes_accessed=2 * 1024 * 1024, transcendentals=0
        ),
        name="sum_z",
    )(*arrays)


def score_kernel(*refs):
    near, far, acts, (own_precond, sib_precond, out) = refs[:4], refs[4], refs[5:9], refs[9:]
    own = jnp.concatenate([b[0] for b in near] + [far[i, 0] for i in range(4)], axis=0)
    sib = jnp.concatenate([b[1] for b in near] + [far[i, 1] for i in range(4)], axis=0)
    acts = [x[...].astype(jnp.float32) for x in acts]
    wide = []
    for dx in range(2):
        for dz in range(4):
            start = (dz * 2 + dx) * ROWS
            wide += [x[start : start + ROWS] for x in acts]
    wide = jnp.concatenate(wide, axis=0)
    for k in range(QUERIES):
        projected = jnp.dot(own, own_precond[k], preferred_element_type=jnp.float32)
        projected += jnp.dot(sib, sib_precond[k], preferred_element_type=jnp.float32)
        out[:, k : k + 1] = jnp.sum(projected * wide, axis=1, keepdims=True)


def score(blocks, acts, own_precond, sib_precond):
    out = pl.pallas_call(
        score_kernel,
        out_shape=jax.ShapeDtypeStruct((GROUP * SEQLEN, QUERIES), jnp.float32),
        in_specs=[VMEM] * 11,
        out_specs=VMEM,
        compiler_params=PARAMS,
        cost_estimate=pl.CostEstimate(
            flops=2 * 512 * 1728 * 1280, bytes_accessed=8 * 1024 * 1024, transcendentals=0
        ),
        name="score",
    )(*blocks, *acts, own_precond, sib_precond)
    return out.reshape(2, 4, GROUP, ROWS, QUERIES)


def act_kernel(order, acts, *refs):
    bases, (kept, other) = refs[:8], refs[8:]
    total = jnp.zeros((acts.shape[1], kept.shape[1]), jnp.float32)
    for m in range(8):
        total += jnp.dot(acts[order[m]], bases[m][...], preferred_element_type=jnp.float32)
    half = acts.shape[1] // 2
    kept[...] = total[:half]
    other[...] = total[half:]


def rotate_acts(order, acts, bases):
    part = jax.ShapeDtypeStruct((acts.shape[1] // 2, bases[0].shape[1]), jnp.float32)
    return pl.pallas_call(
        act_kernel,
        out_shape=(part, part),
        in_specs=[SMEM] + [VMEM] * 9,
        out_specs=(VMEM, VMEM),
        compiler_params=PARAMS,
        cost_estimate=pl.CostEstimate(
            flops=2 * 288 * 2560 * 640, bytes_accessed=6 * 1024 * 1024, transcendentals=0
        ),
        name="rotate_acts",
    )(order, acts, *bases)


def gather_chips(x, hold=None):
    held = {(0, 0): x, (1, 0): take(x, "x_hi", 1)}
    held[0, 1] = take(x, "y", 1)
    held[0, 3] = take(x, "y", -1)
    partner = held[1, 0] if hold is None else after(held[1, 0], hold)
    held[1, 1] = take(partner, "y", 1)
    held[1, 3] = take(partner, "y", -1)
    held[0, 2] = take(held[0, 1], "y", 1)
    held[1, 2] = take(held[1, 3], "y", -1)
    return held


def pad_to(x, *shape, value=0):
    return jnp.pad(x, [(0, n - m) for m, n in zip(x.shape, shape)], constant_values=value)


def per_device(
    train_acts, train_grads, query_acts, query_grads, in_basis, out_basis, eigvals, lengths
):
    x_hi = lax.axis_index("x_hi")
    y = lax.axis_index("y")
    core = lax.axis_index("core")
    x_lo = lax.axis_index("x_lo")
    z = lax.axis_index("z")

    rows_in, rows_out = out_basis.shape
    deep = -(-rows_in // LANES) * LANES
    wide = -(-rows_out // LANES) * LANES
    own_basis = pad_to(out_basis, deep, wide)
    sib_basis = take(own_basis, "core", 1)
    grad_rows = jnp.concatenate(
        [own_rows_first(train_grads, x_lo, z), both_cores(query_grads)[0]], axis=0
    )
    g = gather_chips(pad_to(grad_rows, grad_rows.shape[0], deep))
    groups = (((0, 0), (1, 0), (0, 1), (0, 3)), ((1, 1), (1, 3), (0, 2), (1, 2)))

    half = in_basis.shape[0]
    count = train_acts.shape[0]
    def own_half(x, flip):
        low = (core == 0) != flip
        return jnp.where(low, x[:, :half], x[:, half:])

    sib_acts = take(own_half(train_acts, True), "core", 1)
    chip_acts = jnp.concatenate(
        [
            own_half(train_acts, False),
            own_half(both_cores(query_acts)[0], False),
            sib_acts,
            own_half(both_cores(query_acts)[1], False),
        ],
        axis=0,
    )
    acts = lax.all_gather(chip_acts, TENSOR)
    chips = [(h, d) for h in range(2) for d in range(4)]

    query_parts = {}
    partial = []
    for group in groups:
        *pieces, query = rotate([g[c] for c in group], own_basis, sib_basis)
        query_parts.update((c, query[s]) for s, c in enumerate(group))
        partial.append(pieces)
    bases = gather_chips(after(in_basis, partial[0][0]), partial[1][0])
    sums = []
    rotated = []
    for near, up, down, far_own, far_sib in partial:
        up = up.at[0].add(take(far_own, "z", -1))
        down = down.at[1].add(take(far_sib, "z", 1))
        kept, other = sum_z(near, take(up, "z", -1), take(down, "z", 1))
        sums.append(kept)
        mean = (kept + take(other, "x_lo", 1)).astype(jnp.bfloat16)
        near = [mean] + [take(mean, "z", d) for d in (1, 2, 3)]
        rotated.append(near + [take(jnp.stack(near), "x_lo", 1)])

    order = jnp.stack([(x_hi ^ h) * 4 + (y + d) % 4 for h, d in chips]).astype(jnp.int32)
    kept, other = rotate_acts(order, after(acts, sums[0]), [bases[c] for c in chips])
    rot_acts = (kept + take(other, "core", 1)).astype(jnp.bfloat16)
    rot_acts = jnp.concatenate(
        [own_rows_first(rot_acts[:count], x_lo, z), rot_acts[count:]], axis=0
    )
    shards = gather_chips(rot_acts)

    query_partial = jnp.concatenate([query_parts[c] for c in chips], axis=0)
    pieces = own_rows_first(after(query_partial, sums[0]), x_lo, z).reshape(4, 2, ROWS, -1)
    pieces = pieces[0] + sum(take(pieces[d], "z", -d) for d in (1, 2, 3))
    query_own = (pieces[0] + take(pieces[1], "x_lo", 1)).astype(jnp.bfloat16)
    query_near = jnp.stack([query_own] + [take(query_own, "z", d) for d in (1, 2, 3)])
    query_far = take(query_near, "x_lo", 1)
    query_acts_all = jnp.concatenate([shards[c][count:] for c in chips], axis=0)
    query_acts_all = own_rows_first(after(query_acts_all, sums[1]), x_lo, z).reshape(4, 2, ROWS, -1)
    query_len = 4 * ROWS
    divisor = query_len * (pad_to(eigvals, wide, eigvals.shape[1], value=1.0) + damping)
    precond = []
    for dx, part in enumerate((query_near, query_far)):
        numerator = jnp.dot(
            part.reshape(query_len, -1).T,
            query_acts_all[:, dx].reshape(query_len, -1),
            preferred_element_type=jnp.float32,
        )
        precond.append((numerator / divisor).astype(jnp.bfloat16))
    own_precond = jnp.stack(precond)
    sib_precond = take(own_precond, "core", 1)

    scores = {}
    for group, blocks in zip(groups, rotated):
        result = score(blocks, [shards[c] for c in group], own_precond, sib_precond)
        scores.update((c, result[:, :, s]) for s, c in enumerate(group))
    stacked = jnp.stack([scores[c] for c in chips]).reshape(2, 4, 2, 4, ROWS, QUERIES)
    stacked = stacked.transpose(5, 0, 1, 2, 3, 4)
    stacked = jnp.where(x_lo != x_hi, stacked[::-1], stacked)
    stacked = jnp.where(x_hi == 1, stacked[:, ::-1], stacked)
    stacked = jnp.where(x_lo == 1, stacked[:, :, :, ::-1], stacked)
    stacked = turn(turn(stacked, 2, (-y) % 4), 4, (-z) % 4)
    by_sequence = stacked.reshape(QUERIES, 8, SEQLEN).transpose(1, 0, 2)
    by_core = jnp.stack([jnp.where(core == c, by_sequence, 0.0) for c in range(2)], axis=1)
    spread = jnp.broadcast_to(by_core[:, :, None], (8, 2, 8, QUERIES, SEQLEN))
    received = lax.all_to_all(spread.reshape(128, QUERIES, SEQLEN), AXES, 0, 0, tiled=True)
    raw = jnp.sum(received, axis=0)
    valid = (jnp.arange(SEQLEN, dtype=jnp.int32) < lengths[0]).astype(jnp.float32)
    masked = raw * valid[None, :]
    seq_scores = jnp.sum(masked, axis=1, keepdims=True)
    token_scores = lax.dynamic_slice_in_dim(masked, (x_lo * 4 + z) * ROWS, ROWS, axis=1)
    return (token_scores, seq_scores)


def solution(mesh):
    grid = jax.sharding.Mesh(mesh.devices.reshape(SIZES), AXES)
    dp = AXES[:3]
    return jax.shard_map(
        per_device,
        mesh=grid,
        in_specs=(
            P(dp, TENSOR),
            P(dp, TENSOR),
            P(dp, TENSOR),
            P(dp, TENSOR),
            P(dp, TENSOR),
            P(TENSOR, dp),
            P(dp, TENSOR),
            P(dp),
        ),
        out_specs=(P(None, dp + TENSOR), P(None, dp)),
        check_vma=False,
    )
```

time: 436 us -> 303 us (0.69)
  blocking collectives: 292 us -> 0 us
  waiting for transfers between devices: 44.6 us -> 141 us
  starting transfers between devices: 17.9 us -> 80.4 us
  Pallas kernels: 0 us -> 31.1 us
  matrix products: 32.1 us -> 1.07 us
    psum x2 -> x0, blocking collectives: 251 us -> none  [the longest x1 145 us: per_device(): rotated_grads = lax.psum(grad_partial, 'tensor').astype(jnp.bfloat16)]
    ppermute x0 -> x53, waiting for transfers between devices: none -> 132 us  [take(): lax.ppermute(x, axis, [(i, (i - step) % count) for i in range(count)])]
    ppermute x0 -> x53, starting transfers between devices: none -> 73.4 us  [take(): lax.ppermute(x, axis, [(i, (i - step) % count) for i in range(count)])]
    all_to_all x1 -> x0, blocking collectives: 41.3 us -> none  [per_device(): lax.all_to_all(widened, 'dp', split_axis=1, concat_axis=0, tiled=True)]
    all_gather x2 -> x1, waiting for transfers between devices: 35.3 us -> 0.01 us  [per_device(): acts = lax.all_gather(chip_acts, TENSOR)]
    pallas_call x0 -> x11, Pallas kernels: none -> 31.1 us  [the longest x2 15 us: rotate(): pl.pallas_call(rotate_kernel, out_shape=(pair, pair, pair, single, single...]
    dot_general x4 -> x2, matrix products: 32.1 us -> 1.07 us  [per_device(): jnp.dot(part.reshape(query_len, -1).T, query_acts_all[:, dx].reshape(quer...]
    unnamed x5 -> x101, local copies, waits for them, and re-layouts: 1.23 us -> 19.2 us
  transfers between devices with their start and end apart: 3 -> 55, of which waited for: 2 -> 25; matrix products, arithmetic and copies ran while one was open for 5% -> 4% of each run, Pallas kernels for 0% -> 9%
where the time goes in v2:
time: 303 us; the launch traced here: 302 us
  waiting for transfers between devices  141 us (47%)
  starting transfers between devices  80.4 us (27%)
  Pallas kernels  31.1 us (10%)
  local copies, waits for them, and re-layouts  24 us (8%)
  between operations  15.4 us (5%)
  other arithmetic  9.16 us (3%)
    ppermute x53, waiting for transfers between devices, take(): lax.ppermute(x, axis, [(i, (i - step) % count) for i in range(count)])  132 us
    ppermute x53, starting transfers between devices, take(): lax.ppermute(x, axis, [(i, (i - step) % count) for i in range(count)])  73.4 us
    unnamed x101, local copies, waits for them, and re-layouts  19.2 us
    pallas_call x2, Pallas kernels, rotate(): pl.pallas_call(rotate_kernel, out_shape=(pair, pair, pair, single, single...  15 us
    pallas_call x2, Pallas kernels, score(): pl.pallas_call(score_kernel, out_shape=jax.ShapeDtypeStruct((GROUP * SEQL...  10.6 us
    all_to_all x1, waiting for transfers between devices, per_device(): lax.all_to_all(spread.reshape(128, QUERIES, SEQLEN), AXES, 0, 0, tiled=True)  9.28 us
    all_to_all x1, starting transfers between devices, per_device(): lax.all_to_all(spread.reshape(128, QUERIES, SEQLEN), AXES, 0, 0, tiled=True)  6.92 us
  transfers between devices with their start and end apart: 55, of which 25 were waited for; matrix products, arithmetic and copies ran while one was open for 4% of the time, Pallas kernels for 9%

profile of v2, /device:TPU:1, one launch (start us, length us, event | category | flops | bytes accessed | tf_op | source)
XLA Modules:
  0.0 302.4 jit_solution(17231769118494115904)
XLA Ops:
  22.6 9.5 %collective-permute-done.1.g1 = bf16[144,1792]{1,0:T(8,128)(2,1)} collective-permute-done((bf16[144,1792]{1,0:T(8,128)(2,1)}, bf16[144,1792]{1,0:T(8,128)(2,1)}, u32[]{:S(2)}, u32[]{:S(2)}) %collective-permute-start.1) | collective-permute-done | bytes 516128 | tf_op jit(solution)/shard_map/ppermute | solution.py:28
  40.0 6.2 %collective-permute-done.21.g1 = bf16[144,1792]{1,0:T(8,128)(2,1)} collective-permute-done((bf16[144,1792]{1,0:T(8,128)(2,1)}, bf16[144,1792]{1,0:T(8,128)(2,1)}, u32[]{:S(2)}, u32[]{:S(2)}) %collective-permute-start.21) | collective-permute-done | bytes 516128 | tf_op jit(solution)/shard_map/ppermute | solution.py:28
  47.1 10.2 %collective-permute-done.3.g3 = bf16[144,1792]{1,0:T(8,128)(2,1)} collective-permute-done((bf16[144,1792]{1,0:T(8,128)(2,1)}, bf16[144,1792]{1,0:T(8,128)(2,1)}, u32[]{:S(2)}, u32[]{:S(2)}) %collective-permute-start.3) | collective-permute-done | bytes 516128 | tf_op jit(solution)/shard_map/ppermute | solution.py:28
  57.3 7.0 %rotate.2 = (f32[2,128,896]{2,1,0:T(8,128)S(1)}, f32[2,128,896]{2,1,0:T(8,128)S(1)}, f32[2,128,896]{2,1,0:T(8,128)S(1)}, f32[128,896]{1,0:T(8,128)S(1)}, f32[128...) custom-call(bf16[144,1792]{1,0:T(8,128)(2,1)} %fusion.4.g0, bf16[144,1792]{1,0:T(8,128)(2,1)} %collective-permute-done.1.g1, ...), custom_call_target="tpu_custom_call" | custom-call | flops 3439853568 | bytes 12582912 | tf_op jit(solution)/shard_map/rotate/pallas_call | solution.py:100
  68.4 8.0 %rotate.3 = (f32[2,128,896]{2,1,0:T(8,128)S(1)}, f32[2,128,896]{2,1,0:T(8,128)}, f32[2,128,896]{2,1,0:T(8,128)S(1)}, f32[128,896]{1,0:T(8,128)S(1)}, f32[128,896]{1,0:T(8,128)S(1)}, /*index=5*/f32[4,16,896]{2,1,0:T(8,128)S(1)}) custom-call(bf16[144,1792]{1,0:T(8,128)(2,1)} %collective-permute-done.20.g0, bf16[144,1792]{1,0:T(8,128)(2,1)} %collective-permute-done.21.g1, ...), custom_call_target="tpu_custom_call" | custom-call | flops 3439853568 | bytes 12582912 | tf_op jit(solution)/shard_map/rotate/pallas_call | solution.py:100
  76.4 3.8 %collective-permute-start.44 = (f32[128,896]{1,0:T(8,128)S(1)}, f32[128,896]{1,0:T(8,128)S(1)}, u32[]{:S(2)}, u32[]{:S(2)}) collective-permute-start(f32[128,896]{1,0:T(8,128)S(1)} %get-tuple-element.96), channel_id=1, source_target_pairs={{0,3},{1,0},{2,1},{3,2},{4,7},{5,4},{6,5},{7,6},{8,11},{9,8},{10,9... | collective-permute-start | bytes 1376264 | tf_op jit(solution)/shard_map/ppermute | solution.py:28
  81.7 23.0 %collective-permute-done.7 = f32[128,896]{1,0:T(8,128)S(1)} collective-permute-done((f32[128,896]{1,0:T(8,128)S(1)}, f32[128,896]{1,0:T(8,128)S(1)}, u32[]{:S(2)}, u32[]{:S(2)}) %collective-permute-start.7) | collective-permute-done | bytes 458784 | tf_op jit(solution)/shard_map/ppermute | solution.py:28
  111.3 6.9 %collective-permute-done.25.refs_7_ = bf16[320,640]{1,0:T(8,128)(2,1)S(1)} collective-permute-done((bf16[320,640]{1,0:T(8,128)(2,1)S(1)}, bf16[320,640]{1,0:T(8,128)(2,1)S(1)}, u32[]{:S(2)}, u32[]{:S(2)}) %collective-permute-start.25) | collective-permute-done | bytes 409632 | tf_op jit(solution)/shard_map/ppermute | solution.py:28
  119.9 5.6 %collective-permute-done.8.down = f32[2,128,896]{2,1,0:T(8,128)S(1)} collective-permute-done((f32[2,128,896]{2,1,0:T(8,128)S(1)}, f32[2,128,896]{2,1,0:T(8,128)S(1)}, u32[]{:S(2)}, u32[]{:S(2)}) %collective-permute-start.8) | collective-permute-done | bytes 917536 | tf_op jit(solution)/shard_map/ppermute | solution.py:28
  132.3 6.3 %collective-permute-done.42 = f32[128,896]{1,0:T(8,128)S(1)} collective-permute-done((f32[128,896]{1,0:T(8,128)S(1)}, f32[128,896]{1,0:T(8,128)S(1)}, u32[]{:S(2)}, u32[]{:S(2)}) %collective-permute-start.42) | collective-permute-done | bytes 458784 | tf_op jit(solution)/shard_map/ppermute | solution.py:28
  149.2 7.0 %collective-permute-start.27 = (f32[144,640]{1,0:T(8,128)S(1)}, f32[144,640]{1,0:T(8,128)S(1)}, u32[]{:S(2)}, u32[]{:S(2)}) collective-permute-start(f32[144,640]{1,0:T(8,128)S(1)} %get-tuple-element.89), channel_id=1, source_target_pairs={{0,8},{8,0},{1,9},{9,1},{2,10},{10,2},{3,11},{11,3},{4,12},{12,4},... | collective-permute-start | bytes 1105928 | tf_op jit(solution)/shard_map/ppermute | solution.py:28
  180.3 7.4 %collective-permute-done.41.refs_8_ = bf16[144,640]{1,0:T(8,128)(2,1)S(1)} collective-permute-done((bf16[144,640]{1,0:T(8,128)(2,1)S(1)}, bf16[144,640]{1,0:T(8,128)(2,1)S(1)}, u32[]{:S(2)}, u32[]{:S(2)}) %collective-permute-start.41) | collective-permute-done | bytes 184352 | tf_op jit(solution)/shard_map/ppermute | solution.py:28
  189.8 7.5 %collective-permute-start.47 = (bf16[2,896,640]{2,1,0:T(8,128)(2,1)S(1)}, bf16[2,896,640]{2,1,0:T(8,128)(2,1)}, u32[]{:S(2)}, u32[]{:S(2)}) collective-permute-start(bf16[2,896,640]{2,1,0:T(8,128)(2,1)S(1)} %pad_maximum_fusion.refs_9_), channel_id=1, source_target_pairs={{0,8},{8,0},{1,9},{9,1},{2,10},{10,2},{3,11},{11,3},{4,12},{12,4},... | collective-permute-start | bytes 6881288 | tf_op jit(solution)/shard_map/ppermute | solution.py:28
  198.8 10.3 %collective-permute-done.48 = f32[2,64,896]{2,1,0:T(8,128)S(1)} collective-permute-done((f32[2,64,896]{2,1,0:T(8,128)S(1)}, f32[2,64,896]{2,1,0:T(8,128)S(1)}, u32[]{:S(2)}, u32[]{:S(2)}) %collective-permute-start.48) | collective-permute-done | bytes 458784 | tf_op jit(solution)/shard_map/ppermute | solution.py:28
  210.7 3.7 %collective-permute-done.49.refs_1_ = bf16[2,64,896]{2,1,0:T(8,128)(2,1)S(1)} collective-permute-done((bf16[2,64,896]{2,1,0:T(8,128)(2,1)S(1)}, bf16[2,64,896]{2,1,0:T(8,128)(2,1)S(1)}, u32[]{:S(2)}, u32[]{:S(2)}) %collective-permute-start.49) | collective-permute-done | bytes 229408 | tf_op jit(solution)/shard_map/ppermute | solution.py:28
  215.8 6.9 %collective-permute-done.51.refs_3_ = bf16[2,64,896]{2,1,0:T(8,128)(2,1)S(1)} collective-permute-done((bf16[2,64,896]{2,1,0:T(8,128)(2,1)S(1)}, bf16[2,64,896]{2,1,0:T(8,128)(2,1)S(1)}, u32[]{:S(2)}, u32[]{:S(2)}) %collective-permute-start.51) | collective-permute-done | bytes 229408 | tf_op jit(solution)/shard_map/ppermute | solution.py:28
  226.4 4.6 %collective-permute-done.10.refs_1_ = bf16[2,64,896]{2,1,0:T(8,128)(2,1)S(1)} collective-permute-done((bf16[2,64,896]{2,1,0:T(8,128)(2,1)S(1)}, bf16[2,64,896]{2,1,0:T(8,128)(2,1)S(1)}, u32[]{:S(2)}, u32[]{:S(2)}) %collective-permute-start.10) | collective-permute-done | bytes 229408 | tf_op jit(solution)/shard_map/ppermute | solution.py:28
  232.1 6.9 %collective-permute-done.12.refs_3_ = bf16[2,64,896]{2,1,0:T(8,128)(2,1)S(1)} collective-permute-done((bf16[2,64,896]{2,1,0:T(8,128)(2,1)S(1)}, bf16[2,64,896]{2,1,0:T(8,128)(2,1)S(1)}, u32[]{:S(2)}, u32[]{:S(2)}) %collective-permute-start.12) | collective-permute-done | bytes 229408 | tf_op jit(solution)/shard_map/ppermute | solution.py:28
  240.9 4.0 %collective-permute-done.52.refs_4_ = bf16[4,2,64,896]{3,2,1,0:T(8,128)(2,1)} collective-permute-done((bf16[4,2,64,896]{3,2,1,0:T(8,128)(2,1)}, bf16[4,2,64,896]{3,2,1,0:T(8,128)(2,1)}, u32[]{:S(2)}, u32[]{:S(2)}) %collective-permute-start.52) | collective-permute-done | bytes 917536 | tf_op jit(solution)/shard_map/ppermute | solution.py:28
  250.5 5.3 %score.3 = f32[512,2]{1,0:T(8,128)S(1)} custom-call(bf16[2,64,896]{2,1,0:T(8,128)(2,1)S(1)} %add_convert_fusion.refs_0_, bf16[2,64,896]{2,1,0:T(8,128)(2,1)S(1)} %collective-permute-done.49.refs_1_, bf16[2,64,896]{2,1,0:T(8,128)(2,1)S(1)} %copy-done.9, bf16[2,64,896]{2,1,0:T(8,128)(2,1)S(1)} %copy-done.13, ...), custom_call_target="tpu_custom_call" | custom-call | flops 2264924160 | bytes 8388608 | tf_op jit(solution)/shard_map/score/pallas_call | solution.py:155
  256.3 8.2 %collective-permute-done.13.refs_4_ = bf16[4,2,64,896]{3,2,1,0:T(8,128)(2,1)} collective-permute-done((bf16[4,2,64,896]{3,2,1,0:T(8,128)(2,1)}, bf16[4,2,64,896]{3,2,1,0:T(8,128)(2,1)}, u32[]{:S(2)}, u32[]{:S(2)}) %collective-permute-start.13) | collective-permute-done | bytes 917536 | tf_op jit(solution)/shard_map/ppermute | solution.py:28
  270.1 5.3 %score.2 = f32[512,2]{1,0:T(8,128)S(1)} custom-call(bf16[2,64,896]{2,1,0:T(8,128)(2,1)S(1)} %add_convert_fusion.1.refs_0_, bf16[2,64,896]{2,1,0:T(8,128)(2,1)S(1)} %collective-permute-done.10.refs_1_, bf16[2,64,896]{2,1,0:T(8,128)(2,1)S(1)} %copy-done.11, bf16[2,64,896]{2,1,0:T(8,128)(2,1)S(1)} %copy-done.15, ...), custom_call_target="tpu_custom_call" | custom-call | flops 2264924160 | bytes 8388608 | tf_op jit(solution)/shard_map/score/pallas_call | solution.py:155
  277.3 6.9 %all-to-all-start = ((f32[128,2,128]{2,1,0:T(2,128)}), f32[128,2,128]{2,1,0:T(2,128)S(1)}, u32[]{:S(2)}, u32[]{:S(2)}) async-start(f32[128,2,128]{2,1,0:T(2,128)} %bitcast.72), calls=%async_computation | async-start | bytes 262144 | tf_op jit(solution)/shard_map/all_to_all | solution.py:309
  284.9 9.3 %all-to-all-done = f32[128,2,128]{2,1,0:T(2,128)S(1)} async-done(((f32[128,2,128]{2,1,0:T(2,128)}), f32[128,2,128]{2,1,0:T(2,128)S(1)}, u32[]{:S(2)}, u32[]{:S(2)}) %all-to-all-start) | async-done | bytes 131104 | tf_op jit(solution)/shard_map/all_to_all | solution.py:309
  (249 shorter events, 107.1 us)
Async XLA Ops:
  7.2 134.8 %all-gather.3.cloned.1.call-start = ((), (), s32[]{:S(2)}) async-start(), calls=%async_computation.1 | async-start | bytes 1990656 | tf_op jit(solution)/shard_map/all_gather | solution.py:246
  9.4 47.9 %collective-permute-start.4 = (bf16[1792,896]{1,0:T(8,128)(2,1)S(1)}, bf16[1792,896]{1,0:T(8,128)(2,1)}, u32[]{:S(2)}, u32[]{:S(2)}) collective-permute-start(bf16[1792,896]{1,0:T(8,128)(2,1)S(1)} %pad.21.own_basis), channel_id=1, source_target_pairs={{0,8},{8,0},{1,9},{9,1},{2,10},{10,2},{3,11},{11,3},{4,12},{12,4},... | collective-permute-start | bytes 9633800 | tf_op jit(solution)/shard_map/ppermute | solution.py:28
  19.9 19.9 %collective-permute-start.2 = (bf16[144,1792]{1,0:T(8,128)(2,1)}, bf16[144,1792]{1,0:T(8,128)(2,1)}, u32[]{:S(2)}, u32[]{:S(2)}) collective-permute-start(bf16[144,1792]{1,0:T(8,128)(2,1)} %fusion.4.g0), channel_id=1, source_target_pairs={{0,48},{16,0},{32,16},{48,32},{1,49},{17,1},{33,17},{49,33},{2,50}... | collective-permute-start | bytes 1548296 | tf_op jit(solution)/shard_map/ppermute | solution.py:28
  34.7 22.6 %collective-permute-start.3 = (bf16[144,1792]{1,0:T(8,128)(2,1)}, bf16[144,1792]{1,0:T(8,128)(2,1)}, u32[]{:S(2)}, u32[]{:S(2)}) collective-permute-start(bf16[144,1792]{1,0:T(8,128)(2,1)} %fusion.4.g0), channel_id=1, source_target_pairs={{0,16},{16,32},{32,48},{48,0},{1,17},{17,33},{33,49},{49,1},{2,18}... | collective-permute-start | bytes 1548296 | tf_op jit(solution)/shard_map/ppermute | solution.py:28
  38.4 30.0 %collective-permute-start.20 = (bf16[144,1792]{1,0:T(8,128)(2,1)}, bf16[144,1792]{1,0:T(8,128)(2,1)}, u32[]{:S(2)}, u32[]{:S(2)}) collective-permute-start(bf16[144,1792]{1,0:T(8,128)(2,1)} %collective-permute-done.1.g1), channel_id=1, source_target_pairs={{0,48},{16,0},{32,16},{48,32},{1,49},{17,1},{33,17},{49,33},{2,50}... | collective-permute-start | bytes 1548296 | tf_op jit(solution)/shard_map/ppermute | solution.py:28
  39.8 28.6 %collective-permute-start.22 = (bf16[144,1792]{1,0:T(8,128)(2,1)}, bf16[144,1792]{1,0:T(8,128)(2,1)}, u32[]{:S(2)}, u32[]{:S(2)}) collective-permute-start(bf16[144,1792]{1,0:T(8,128)(2,1)} %collective-permute-done.2.g2), channel_id=1, source_target_pairs={{0,48},{16,0},{32,16},{48,32},{1,49},{17,1},{33,17},{49,33},{2,50}... | collective-permute-start | bytes 1548296 | tf_op jit(solution)/shard_map/ppermute | solution.py:28
  46.2 22.2 %collective-permute-start.23 = (bf16[144,1792]{1,0:T(8,128)(2,1)}, bf16[144,1792]{1,0:T(8,128)(2,1)}, u32[]{:S(2)}, u32[]{:S(2)}) collective-permute-start(bf16[144,1792]{1,0:T(8,128)(2,1)} %collective-permute-done.21.g1), channel_id=1, source_target_pairs={{0,16},{16,32},{32,48},{48,0},{1,17},{17,33},{33,49},{49,1},{2,18}... | collective-permute-start | bytes 1548296 | tf_op jit(solution)/shard_map/ppermute | solution.py:28
  64.3 44.2 %collective-permute-start.19 = (bf16[320,640]{1,0:T(8,128)(2,1)S(1)}, bf16[320,640]{1,0:T(8,128)(2,1)S(1)}, u32[]{:S(2)}, u32[]{:S(2)}) collective-permute-start(bf16[320,640]{1,0:T(8,128)(2,1)S(1)} %copy-done.4), channel_id=1, source_target_pairs={{0,64},{64,0},{1,65},{65,1},{2,66},{66,2},{3,67},{67,3},{4,68},{68... | collective-permute-start | bytes 1228808 | tf_op jit(solution)/shard_map/ppermute | solution.py:28
  67.0 42.8 %collective-permute-start.16 = (bf16[320,640]{1,0:T(8,128)(2,1)S(1)}, bf16[320,640]{1,0:T(8,128)(2,1)}, u32[]{:S(2)}, u32[]{:S(2)}) collective-permute-start(bf16[320,640]{1,0:T(8,128)(2,1)S(1)} %copy-done.4), channel_id=1, source_target_pairs={{0,48},{16,0},{32,16},{48,32},{1,49},{17,1},{33,17},{49,33},{2,50}... | collective-permute-start | bytes 1228808 | tf_op jit(solution)/shard_map/ppermute | solution.py:28
  76.4 34.9 %collective-permute-start.44 = (f32[128,896]{1,0:T(8,128)S(1)}, f32[128,896]{1,0:T(8,128)S(1)}, u32[]{:S(2)}, u32[]{:S(2)}) collective-permute-start(f32[128,896]{1,0:T(8,128)S(1)} %get-tuple-element.96), channel_id=1, source_target_pairs={{0,3},{1,0},{2,1},{3,2},{4,7},{5,4},{6,5},{7,6},{8,11},{9,8},{10,9... | collective-permute-start | bytes 1376264 | tf_op jit(solution)/shard_map/ppermute | solution.py:28
  80.1 24.5 %collective-permute-start.7 = (f32[128,896]{1,0:T(8,128)S(1)}, f32[128,896]{1,0:T(8,128)S(1)}, u32[]{:S(2)}, u32[]{:S(2)}) collective-permute-start(f32[128,896]{1,0:T(8,128)S(1)} %get-tuple-element.79), channel_id=1, source_target_pairs={{0,3},{1,0},{2,1},{3,2},{4,7},{5,4},{6,5},{7,6},{8,11},{9,8},{10,9... | collective-permute-start | bytes 1376264 | tf_op jit(solution)/shard_map/ppermute | solution.py:28
  80.3 28.0 %collective-permute-start.5 = (f32[128,896]{1,0:T(8,128)S(1)}, f32[128,896]{1,0:T(8,128)S(1)}, u32[]{:S(2)}, u32[]{:S(2)}) collective-permute-start(f32[128,896]{1,0:T(8,128)S(1)} %get-tuple-element.77), channel_id=1, source_target_pairs={{0,1},{1,2},{2,3},{3,0},{4,5},{5,6},{6,7},{7,4},{8,9},{9,10},{10,1... | collective-permute-start | bytes 1376264 | tf_op jit(solution)/shard_map/ppermute | solution.py:28
  104.8 20.7 %collective-permute-start.8 = (f32[2,128,896]{2,1,0:T(8,128)S(1)}, f32[2,128,896]{2,1,0:T(8,128)S(1)}, u32[]{:S(2)}, u32[]{:S(2)}) collective-permute-start(f32[2,128,896]{2,1,0:T(8,128)S(1)} %fusion.7), channel_id=1, source_target_pairs={{0,3},{1,0},{2,1},{3,2},{4,7},{5,4},{6,5},{7,6},{8,11},{9,8},{10,9... | collective-permute-start | bytes 2752520 | tf_op jit(solution)/shard_map/ppermute | solution.py:28
  108.4 20.4 %collective-permute-start.6 = (f32[2,128,896]{2,1,0:T(8,128)S(1)}, f32[2,128,896]{2,1,0:T(8,128)S(1)}, u32[]{:S(2)}, u32[]{:S(2)}) collective-permute-start(f32[2,128,896]{2,1,0:T(8,128)S(1)} %fusion.8), channel_id=1, source_target_pairs={{0,1},{1,2},{2,3},{3,0},{4,5},{5,6},{6,7},{7,4},{8,9},{9,10},{10,1... | collective-permute-start | bytes 2752520 | tf_op jit(solution)/shard_map/ppermute | solution.py:28
  109.8 22.5 %collective-permute-start.18 = (bf16[320,640]{1,0:T(8,128)(2,1)S(1)}, bf16[320,640]{1,0:T(8,128)(2,1)S(1)}, u32[]{:S(2)}, u32[]{:S(2)}) collective-permute-start(bf16[320,640]{1,0:T(8,128)(2,1)S(1)} %copy-done.4), channel_id=1, source_target_pairs={{0,16},{16,32},{32,48},{48,0},{1,17},{17,33},{33,49},{49,1},{2,18}... | collective-permute-start | bytes 1228808 | tf_op jit(solution)/shard_map/ppermute | solution.py:28
  111.3 27.3 %collective-permute-start.42 = (f32[128,896]{1,0:T(8,128)S(1)}, f32[128,896]{1,0:T(8,128)S(1)}, u32[]{:S(2)}, u32[]{:S(2)}) collective-permute-start(f32[128,896]{1,0:T(8,128)S(1)} %get-tuple-element.94), channel_id=1, source_target_pairs={{0,1},{1,2},{2,3},{3,0},{4,5},{5,6},{6,7},{7,4},{8,9},{9,10},{10,1... | collective-permute-start | bytes 1376264 | tf_op jit(solution)/shard_map/ppermute | solution.py:28
  118.2 20.4 %collective-permute-start.24 = (bf16[320,640]{1,0:T(8,128)(2,1)S(1)}, bf16[320,640]{1,0:T(8,128)(2,1)S(1)}, u32[]{:S(2)}, u32[]{:S(2)}) collective-permute-start(bf16[320,640]{1,0:T(8,128)(2,1)S(1)} %collective-permute-done.19.refs_4_), channel_id=1, source_target_pairs={{0,48},{16,0},{32,16},{48,32},{1,49},{17,1},{33,17},{49,33},{2,50}... | collective-permute-start | bytes 1228808 | tf_op jit(solution)/shard_map/ppermute | solution.py:28
  141.9 24.3 %collective-permute-start.45 = (f32[2,128,896]{2,1,0:T(8,128)}, f32[2,128,896]{2,1,0:T(8,128)S(1)}, u32[]{:S(2)}, u32[]{:S(2)}) collective-permute-start(f32[2,128,896]{2,1,0:T(8,128)} %copy-done.16), channel_id=1, source_target_pairs={{0,3},{1,0},{2,1},{3,2},{4,7},{5,4},{6,5},{7,6},{8,11},{9,8},{10,9... | collective-permute-start | bytes 2752520 | tf_op jit(solution)/shard_map/ppermute | solution.py:28
  143.7 22.5 %collective-permute-start.43 = (f32[2,128,896]{2,1,0:T(8,128)}, f32[2,128,896]{2,1,0:T(8,128)S(1)}, u32[]{:S(2)}, u32[]{:S(2)}) collective-permute-start(f32[2,128,896]{2,1,0:T(8,128)} %fusion.6), channel_id=1, source_target_pairs={{0,1},{1,2},{2,3},{3,0},{4,5},{5,6},{6,7},{7,4},{8,9},{9,10},{10,1... | collective-permute-start | bytes 2752520 | tf_op jit(solution)/shard_map/ppermute | solution.py:28
  170.6 18.4 %collective-permute-start.46 = (bf16[4,16,896]{2,1,0:T(8,128)(2,1)S(1)}, bf16[4,16,896]{2,1,0:T(8,128)(2,1)S(1)}, u32[]{:S(2)}, u32[]{:S(2)}) collective-permute-start(bf16[4,16,896]{2,1,0:T(8,128)(2,1)S(1)} %pad_maximum_fusion.6), channel_id=1, source_target_pairs={{0,4},{4,0},{1,5},{5,1},{2,6},{6,2},{3,7},{7,3},{8,12},{12,8},{9,1... | collective-permute-start | bytes 344072 | tf_op jit(solution)/shard_map/ppermute | solution.py:28
  189.8 55.1 %collective-permute-start.47 = (bf16[2,896,640]{2,1,0:T(8,128)(2,1)S(1)}, bf16[2,896,640]{2,1,0:T(8,128)(2,1)}, u32[]{:S(2)}, u32[]{:S(2)}) collective-permute-start(bf16[2,896,640]{2,1,0:T(8,128)(2,1)S(1)} %pad_maximum_fusion.refs_9_), channel_id=1, source_target_pairs={{0,8},{8,0},{1,9},{9,1},{2,10},{10,2},{3,11},{11,3},{4,12},{12,4},... | collective-permute-start | bytes 6881288 | tf_op jit(solution)/shard_map/ppermute | solution.py:28
  197.4 27.4 %collective-permute-start.9 = (f32[2,64,896]{2,1,0:T(8,128)S(1)}, f32[2,64,896]{2,1,0:T(8,128)S(1)}, u32[]{:S(2)}, u32[]{:S(2)}) collective-permute-start(f32[2,64,896]{2,1,0:T(8,128)S(1)} %copy-done.34), channel_id=1, source_target_pairs={{0,4},{4,0},{1,5},{5,1},{2,6},{6,2},{3,7},{7,3},{8,12},{12,8},{9,1... | collective-permute-start | bytes 1376264 | tf_op jit(solution)/shard_map/ppermute | solution.py:28
  223.8 21.1 %collective-permute-start.52 = (bf16[4,2,64,896]{3,2,1,0:T(8,128)(2,1)}, bf16[4,2,64,896]{3,2,1,0:T(8,128)(2,1)}, u32[]{:S(2)}, u32[]{:S(2)}) collective-permute-start(bf16[4,2,64,896]{3,2,1,0:T(8,128)(2,1)} %pad_maximum_fusion.2), channel_id=1, source_target_pairs={{0,4},{4,0},{1,5},{5,1},{2,6},{6,2},{3,7},{7,3},{8,12},{12,8},{9,1... | collective-permute-start | bytes 2752520 | tf_op jit(solution)/shard_map/ppermute | solution.py:28
  240.9 23.6 %collective-permute-start.13 = (bf16[4,2,64,896]{3,2,1,0:T(8,128)(2,1)}, bf16[4,2,64,896]{3,2,1,0:T(8,128)(2,1)}, u32[]{:S(2)}, u32[]{:S(2)}) collective-permute-start(bf16[4,2,64,896]{3,2,1,0:T(8,128)(2,1)} %pad_maximum_fusion.1), channel_id=1, source_target_pairs={{0,4},{4,0},{1,5},{5,1},{2,6},{6,2},{3,7},{7,3},{8,12},{12,8},{9,1... | collective-permute-start | bytes 2752520 | tf_op jit(solution)/shard_map/ppermute | solution.py:28
  (70 other events, 693.4 us)
Sparse Core Ops, SparseCore 0:
  47.2 44.6 all-gather.2

commit v3 on v2

--- a/solution.py
+++ b/solution.py
@@ -14,10 +14,12 @@
 ROWS = 16
 LANES = 128
 GROUP = 4
-VMEM_BYTES = 24 * 1024 * 1024
 VMEM = pl.BlockSpec(memory_space=pltpu.VMEM)
 SMEM = pl.BlockSpec(memory_space=pltpu.SMEM)
-PARAMS = pltpu.CompilerParams(vmem_limit_bytes=VMEM_BYTES)
+
+
+def params(mib):
+    return pltpu.CompilerParams(vmem_limit_bytes=mib * 1024 * 1024)
 
 
 damping = 0.1
@@ -50,7 +52,7 @@
         out_shape=jax.ShapeDtypeStruct(blocks.shape, blocks.dtype),
         in_specs=[SMEM, VMEM],
         out_specs=VMEM,
-        compiler_params=PARAMS,
+        compiler_params=params(6),
         name="pick",
     )(order, blocks)
 
@@ -102,7 +104,7 @@
         out_shape=(pair, pair, pair, single, single, query),
         in_specs=[VMEM] * 6,
         out_specs=(VMEM,) * 6,
-        compiler_params=PARAMS,
+        compiler_params=params(24),
         cost_estimate=pl.CostEstimate(
             flops=2 * 576 * 1728 * 1728, bytes_accessed=12 * 1024 * 1024, transcendentals=0
         ),
@@ -126,7 +128,7 @@
         out_shape=(part, part),
         in_specs=[VMEM] * 3,
         out_specs=(VMEM, VMEM),
-        compiler_params=PARAMS,
+        compiler_params=params(10),
         cost_estimate=pl.CostEstimate(
             flops=4 * 64 * 864, bytes_accessed=2 * 1024 * 1024, transcendentals=0
         ),
@@ -135,9 +137,13 @@
 
 
 def score_kernel(*refs):
-    near, far, acts, (own_precond, sib_precond, out) = refs[:4], refs[4], refs[5:9], refs[9:]
-    own = jnp.concatenate([b[0] for b in near] + [far[i, 0] for i in range(4)], axis=0)
-    sib = jnp.concatenate([b[1] for b in near] + [far[i, 1] for i in range(4)], axis=0)
+    blocks, acts, (own_precond, sib_precond, out) = refs[:-7], refs[-7:-3], refs[-3:]
+    if len(blocks) == 5:
+        place = [b for b in blocks[:4]] + [blocks[4].at[i] for i in range(4)]
+    else:
+        place = [b.at[dx] for dx in range(2) for b in blocks]
+    own = jnp.concatenate([b[0] for b in place], axis=0)
+    sib = jnp.concatenate([b[1] for b in place], axis=0)
     acts = [x[...].astype(jnp.float32) for x in acts]
     wide = []
     for dx in range(2):
@@ -155,9 +161,9 @@
     out = pl.pallas_call(
         score_kernel,
         out_shape=jax.ShapeDtypeStruct((GROUP * SEQLEN, QUERIES), jnp.float32),
-        in_specs=[VMEM] * 11,
+        in_specs=[VMEM] * (len(blocks) + 6),
         out_specs=VMEM,
-        compiler_params=PARAMS,
+        compiler_params=params(20),
         cost_estimate=pl.CostEstimate(
             flops=2 * 512 * 1728 * 1280, bytes_accessed=8 * 1024 * 1024, transcendentals=0
         ),
@@ -183,24 +189,12 @@
         out_shape=(part, part),
         in_specs=[SMEM] + [VMEM] * 9,
         out_specs=(VMEM, VMEM),
-        compiler_params=PARAMS,
+        compiler_params=params(12),
         cost_estimate=pl.CostEstimate(
             flops=2 * 288 * 2560 * 640, bytes_accessed=6 * 1024 * 1024, transcendentals=0
         ),
         name="rotate_acts",
     )(order, acts, *bases)
-
-
-def gather_chips(x, hold=None):
-    held = {(0, 0): x, (1, 0): take(x, "x_hi", 1)}
-    held[0, 1] = take(x, "y", 1)
-    held[0, 3] = take(x, "y", -1)
-    partner = held[1, 0] if hold is None else after(held[1, 0], hold)
-    held[1, 1] = take(partner, "y", 1)
-    held[1, 3] = take(partner, "y", -1)
-    held[0, 2] = take(held[0, 1], "y", 1)
-    held[1, 2] = take(held[1, 3], "y", -1)
-    return held
 
 
 def pad_to(x, *shape, value=0):
@@ -215,17 +209,6 @@
     core = lax.axis_index("core")
     x_lo = lax.axis_index("x_lo")
     z = lax.axis_index("z")
-
-    rows_in, rows_out = out_basis.shape
-    deep = -(-rows_in // LANES) * LANES
-    wide = -(-rows_out // LANES) * LANES
-    own_basis = pad_to(out_basis, deep, wide)
-    sib_basis = take(own_basis, "core", 1)
-    grad_rows = jnp.concatenate(
-        [own_rows_first(train_grads, x_lo, z), both_cores(query_grads)[0]], axis=0
-    )
-    g = gather_chips(pad_to(grad_rows, grad_rows.shape[0], deep))
-    groups = (((0, 0), (1, 0), (0, 1), (0, 3)), ((1, 1), (1, 3), (0, 2), (1, 2)))
 
     half = in_basis.shape[0]
     count = train_acts.shape[0]
@@ -243,43 +226,115 @@
         ],
         axis=0,
     )
-    acts = lax.all_gather(chip_acts, TENSOR)
+    sync = lax.optimization_barrier
+    rows_in, rows_out = out_basis.shape
+    deep = -(-rows_in // LANES) * LANES
+    wide = -(-rows_out // LANES) * LANES
+    own_basis = pad_to(out_basis, deep, wide)
+    grad_rows = jnp.concatenate(
+        [own_rows_first(train_grads, x_lo, z), both_cores(query_grads)[0]], axis=0
+    )
+    g = {(0, 0): pad_to(grad_rows, grad_rows.shape[0], deep)}
+    g[1, 0] = take(g[0, 0], "x_hi", 1)
+    g[0, 1] = take(g[0, 0], "y", 1)
+    g[0, 3] = take(g[0, 0], "y", -1)
+    sib_basis = take(own_basis, "core", 1)
+    acts_z = [take(chip_acts, "z", d) for d in (1, 2, 3)]
+    g[1, 0], g[0, 1], g[0, 3], sib_basis, acts_z = sync(
+        (g[1, 0], g[0, 1], g[0, 3], sib_basis, acts_z)
+    )
     chips = [(h, d) for h in range(2) for d in range(4)]
-
-    query_parts = {}
-    partial = []
-    for group in groups:
-        *pieces, query = rotate([g[c] for c in group], own_basis, sib_basis)
-        query_parts.update((c, query[s]) for s, c in enumerate(group))
-        partial.append(pieces)
-    bases = gather_chips(after(in_basis, partial[0][0]), partial[1][0])
-    sums = []
-    rotated = []
-    for near, up, down, far_own, far_sib in partial:
-        up = up.at[0].add(take(far_own, "z", -1))
-        down = down.at[1].add(take(far_sib, "z", 1))
-        kept, other = sum_z(near, take(up, "z", -1), take(down, "z", 1))
-        sums.append(kept)
-        mean = (kept + take(other, "x_lo", 1)).astype(jnp.bfloat16)
-        near = [mean] + [take(mean, "z", d) for d in (1, 2, 3)]
-        rotated.append(near + [take(jnp.stack(near), "x_lo", 1)])
-
-    order = jnp.stack([(x_hi ^ h) * 4 + (y + d) % 4 for h, d in chips]).astype(jnp.int32)
-    kept, other = rotate_acts(order, after(acts, sums[0]), [bases[c] for c in chips])
+    groups = (((0, 0), (1, 0), (0, 1), (0, 3)), ((1, 1), (1, 3), (0, 2), (1, 2)))
+
+    g[1, 1] = take(g[1, 0], "y", 1)
+    g[1, 3] = take(g[1, 0], "y", -1)
+    near_1, up_1, down_1, far_own, far_sib, query_1 = rotate(
+        [g[c] for c in groups[0]], own_basis, sib_basis
+    )
+    g[1, 1], g[1, 3], near_1, up_1, down_1, far_own, far_sib, query_1 = sync(
+        (g[1, 1], g[1, 3], near_1, up_1, down_1, far_own, far_sib, query_1)
+    )
+
+    far_own, far_sib = take(far_own, "z", -1), take(far_sib, "z", 1)
+    g[0, 2] = take(g[0, 1], "y", 1)
+    g[1, 2] = take(g[1, 3], "y", -1)
+    acts_near = jnp.stack([chip_acts] + acts_z)
+    acts_far = take(acts_near, "x_lo", 1)
+    far_own, far_sib, g[0, 2], g[1, 2] = sync((far_own, far_sib, g[0, 2], g[1, 2]))
+
+    up_1 = take(up_1.at[0].add(far_own), "z", -1)
+    down_1 = take(down_1.at[1].add(far_sib), "z", 1)
+    v = {(0, 0): sync((in_basis, g[1, 2]))[0]}
+    v[1, 0] = take(v[0, 0], "x_hi", 1)
+    v[0, 1] = take(v[0, 0], "y", 1)
+    v[0, 3] = take(v[0, 0], "y", -1)
+    near_2, up_2, down_2, far_own, far_sib, query_2 = rotate(
+        [g[c] for c in groups[1]], own_basis, sib_basis
+    )
+    far_own, far_sib = take(far_own, "z", -1), take(far_sib, "z", 1)
+    query_parts = {c: query_1[s] for s, c in enumerate(groups[0])}
+    query_parts.update((c, query_2[s]) for s, c in enumerate(groups[1]))
+    query_partial = jnp.concatenate([query_parts[c] for c in chips], axis=0)
+    pieces = own_rows_first(query_partial, x_lo, z).reshape(4, 2, ROWS, -1)
+    query_z = [take(pieces[d], "z", -d) for d in (1, 2, 3)]
+    (up_1, down_1, v[1, 0], v[0, 1], v[0, 3], near_2, up_2, down_2, far_own, far_sib, query_z, acts_far) = sync(
+        (up_1, down_1, v[1, 0], v[0, 1], v[0, 3], near_2, up_2, down_2, far_own, far_sib, query_z, acts_far)
+    )
+
+    up_2 = take(up_2.at[0].add(far_own), "z", -1)
+    down_2 = take(down_2.at[1].add(far_sib), "z", 1)
+    kept_1, other_1 = sum_z(near_1, up_1, down_1)
+    other_1 = take(other_1, "x_lo", 1)
+    v[1, 1] = take(v[1, 0], "y", 1)
+    v[1, 3] = take(v[1, 0], "y", -1)
+    v[0, 2] = take(v[0, 1], "y", 1)
+    v[1, 2] = take(v[1, 3], "y", -1)
+    pieces = pieces[0] + query_z[0] + query_z[1] + query_z[2]
+    query_x = take(pieces[1], "x_lo", 1)
+    acts = jnp.concatenate([acts_near, acts_far], axis=0)
+    (up_2, down_2, kept_1, other_1, v[1, 1], v[1, 3], v[0, 2], v[1, 2], query_x, acts) = sync(
+        (up_2, down_2, kept_1, other_1, v[1, 1], v[1, 3], v[0, 2], v[1, 2], query_x, acts)
+    )
+
+    mean_1 = (kept_1 + other_1).astype(jnp.bfloat16)
+    kept_2, other_2 = sum_z(near_2, up_2, down_2)
+    other_2 = take(other_2, "x_lo", 1)
+    near_1 = [take(mean_1, "z", d) for d in (1, 2, 3)]
+    order = jnp.stack([(x_lo ^ x_hi ^ h) * 4 + (y - z + d) % 4 for h, d in chips])
+    kept, other = rotate_acts(order.astype(jnp.int32), acts, [v[c] for c in chips])
     rot_acts = (kept + take(other, "core", 1)).astype(jnp.bfloat16)
     rot_acts = jnp.concatenate(
         [own_rows_first(rot_acts[:count], x_lo, z), rot_acts[count:]], axis=0
     )
-    shards = gather_chips(rot_acts)
-
-    query_partial = jnp.concatenate([query_parts[c] for c in chips], axis=0)
-    pieces = own_rows_first(after(query_partial, sums[0]), x_lo, z).reshape(4, 2, ROWS, -1)
-    pieces = pieces[0] + sum(take(pieces[d], "z", -d) for d in (1, 2, 3))
-    query_own = (pieces[0] + take(pieces[1], "x_lo", 1)).astype(jnp.bfloat16)
-    query_near = jnp.stack([query_own] + [take(query_own, "z", d) for d in (1, 2, 3)])
+    r = {(0, 0): rot_acts}
+    r[1, 0] = take(r[0, 0], "x_hi", 1)
+    r[0, 1] = take(r[0, 0], "y", 1)
+    r[0, 3] = take(r[0, 0], "y", -1)
+    query_own = (pieces[0] + query_x).astype(jnp.bfloat16)
+    query_near = [take(query_own, "z", d) for d in (1, 2, 3)]
+    kept_2, other_2, near_1, r[1, 0], r[0, 1], r[0, 3], query_near = sync(
+        (kept_2, other_2, near_1, r[1, 0], r[0, 1], r[0, 3], query_near)
+    )
+
+    mean_2 = (kept_2 + other_2).astype(jnp.bfloat16)
+    pair_2 = take(mean_2, "x_lo", 1)
+    query_near = jnp.stack([query_own] + query_near)
     query_far = take(query_near, "x_lo", 1)
-    query_acts_all = jnp.concatenate([shards[c][count:] for c in chips], axis=0)
-    query_acts_all = own_rows_first(after(query_acts_all, sums[1]), x_lo, z).reshape(4, 2, ROWS, -1)
+    r[1, 1] = take(r[1, 0], "y", 1)
+    r[1, 3] = take(r[1, 0], "y", -1)
+    r[0, 2] = take(r[0, 1], "y", 1)
+    r[1, 2] = take(r[1, 3], "y", -1)
+    near_1 = [mean_1] + near_1
+    near_1_all = jnp.stack(near_1)
+    pair_2, query_far, r[1, 1], r[1, 3], r[0, 2], r[1, 2], near_1_all = sync(
+        (pair_2, query_far, r[1, 1], r[1, 3], r[0, 2], r[1, 2], near_1_all)
+    )
+
+    far_1 = take(near_1_all, "x_lo", 1)
+    pair_2 = jnp.stack([mean_2, pair_2])
+    pairs_2 = [pair_2] + [take(pair_2, "z", d) for d in (1, 2, 3)]
+    query_acts_all = jnp.concatenate([r[c][count:] for c in chips], axis=0)
+    query_acts_all = own_rows_first(query_acts_all, x_lo, z).reshape(4, 2, ROWS, -1)
     query_len = 4 * ROWS
     divisor = query_len * (pad_to(eigvals, wide, eigvals.shape[1], value=1.0) + damping)
     precond = []
@@ -292,6 +347,9 @@
         precond.append((numerator / divisor).astype(jnp.bfloat16))
     own_precond = jnp.stack(precond)
     sib_precond = take(own_precond, "core", 1)
+    far_1, pairs_2, sib_precond = sync((far_1, pairs_2, sib_precond))
+    shards = r
+    rotated = (near_1 + [far_1], pairs_2)
 
     scores = {}
     for group, blocks in zip(groups, rotated):

time: 303 us -> 259 us (0.85)
  waiting for transfers between devices: 141 us -> 110 us
  between operations: 15.4 us -> 2.05 us
  local copies, waits for them, and re-layouts: 24 us -> 18.5 us
    ppermute x53 -> x57, waiting for transfers between devices: 132 us -> 101 us  [take(): lax.ppermute(x, axis, [(i, (i - step) % count) for i in range(count)])]
    unnamed x101 -> x112, local copies, waits for them, and re-layouts: 19.2 us -> 14.2 us
    scatter-add x4, other arithmetic: 2.16 us -> 6.9 us  [the longest x1 1.99 us: per_device(): up_2 = take(up_2.at[0].add(far_own), 'z', -1)]
    ppermute x53 -> x57, starting transfers between devices: 73.4 us -> 75.8 us  [take(): lax.ppermute(x, axis, [(i, (i - step) % count) for i in range(count)])]
  transfers between devices with their start and end apart: 55 -> 58, of which waited for: 25 -> 29; matrix products, arithmetic and copies ran while one was open for 4% -> 5% of each run, Pallas kernels for 9% -> 7%
where the time goes in v3:
time: 259 us; the launch traced here: 258 us
  waiting for transfers between devices  110 us (42%)
  starting transfers between devices  82.2 us (32%)
  Pallas kernels  32.9 us (13%)
  local copies, waits for them, and re-layouts  18.5 us (7%)
  other arithmetic  11.5 us (4%)
    ppermute x57, waiting for transfers between devices, take(): lax.ppermute(x, axis, [(i, (i - step) % count) for i in range(count)])  101 us
    ppermute x57, starting transfers between devices, take(): lax.ppermute(x, axis, [(i, (i - step) % count) for i in range(count)])  75.8 us
    pallas_call x2, Pallas kernels, rotate(): pl.pallas_call(rotate_kernel, out_shape=(pair, pair, pair, single, single...  14.8 us
    unnamed x112, local copies, waits for them, and re-layouts  14.2 us
    pallas_call x2, Pallas kernels, score(): pl.pallas_call(score_kernel, out_shape=jax.ShapeDtypeStruct((GROUP * SEQL...  10.9 us
    all_to_all x1, waiting for transfers between devices, per_device(): lax.all_to_all(spread.reshape(128, QUERIES, SEQLEN), AXES, 0, 0, tiled=True)  9.28 us
    all_to_all x1, starting transfers between devices, per_device(): lax.all_to_all(spread.reshape(128, QUERIES, SEQLEN), AXES, 0, 0, tiled=True)  6.35 us
  transfers between devices with their start and end apart: 58, of which 29 were waited for; matrix products, arithmetic and copies ran while one was open for 5% of the time, Pallas kernels for 7%

profile of v3, /device:TPU:1, one launch (start us, length us, event | category | flops | bytes accessed | tf_op | source)
XLA Modules:
  0.0 258.4 jit_solution(5140993893322898674)
XLA Ops:
  10.9 3.9 %collective-permute-start.7 = (bf16[288,320]{1,0:T(8,128)(2,1)S(1)}, bf16[288,320]{1,0:T(8,128)(2,1)S(1)}, u32[]{:S(2)}, u32[]{:S(2)}) collective-permute-start(bf16[288,320]{1,0:T(8,128)(2,1)S(1)} %get-tuple-element.240), channel_id=1, source_target_pairs={{0,3},{1,0},{2,1},{3,2},{4,7},{5,4},{6,5},{7,6},{8,11},{9,8},{10,9... | collective-permute-start | bytes 552968 | tf_op jit(solution)/shard_map/ppermute | solution.py:30
  21.5 6.4 %collective-permute-done.8 = bf16[288,320]{1,0:T(8,128)(2,1)S(1)} collective-permute-done((bf16[288,320]{1,0:T(8,128)(2,1)S(1)}, bf16[288,320]{1,0:T(8,128)(2,1)S(1)}, u32[]{:S(2)}, u32[]{:S(2)}) %collective-permute-start.8) | collective-permute-done | bytes 184352 | tf_op jit(solution)/shard_map/ppermute | solution.py:30
  28.3 5.9 %collective-permute-done.9 = bf16[288,320]{1,0:T(8,128)(2,1)S(1)} collective-permute-done((bf16[288,320]{1,0:T(8,128)(2,1)S(1)}, bf16[288,320]{1,0:T(8,128)(2,1)S(1)}, u32[]{:S(2)}, u32[]{:S(2)}) %collective-permute-start.9) | collective-permute-done | bytes 184352 | tf_op jit(solution)/shard_map/ppermute | solution.py:30
  39.2 7.6 %rotate.2 = (f32[2,128,896]{2,1,0:T(8,128)S(1)}, f32[2,128,896]{2,1,0:T(8,128)}, f32[2,128,896]{2,1,0:T(8,128)}, f32[128,896]{1,0:T(8,128)S(1)}, f32[128,896]{1,0:T(8,128)S(1)}, /*index=5*/f32[4,16,896]{2,1,0:T(8,128)S(1)}) custom-call(bf16[144,1792]{1,0:T(8,128)(2,1)S(1)} %fusion.4.g0, bf16[144,1792]{1,0:T(8,128)(2,1)S(1)} %collective-permute-done.1.g1, ...), custom_call_target="tpu_custom_call" | custom-call | flops 3439853568 | bytes 12582912 | tf_op jit(solution)/shard_map/rotate/pallas_call | solution.py:102
  56.2 3.4 %collective-permute-done.15.g3 = bf16[144,1792]{1,0:T(8,128)(2,1)S(1)} collective-permute-done((bf16[144,1792]{1,0:T(8,128)(2,1)S(1)}, bf16[144,1792]{1,0:T(8,128)(2,1)S(1)}, u32[]{:S(2)}, u32[]{:S(2)}) %collective-permute-start.15) | collective-permute-done | bytes 516128 | tf_op jit(solution)/shard_map/ppermute | solution.py:30
  59.6 4.7 %collective-permute-start.18 = (bf16[320,640]{1,0:T(8,128)(2,1)}, bf16[320,640]{1,0:T(8,128)(2,1)}, u32[]{:S(2)}, u32[]{:S(2)}) collective-permute-start(bf16[320,640]{1,0:T(8,128)(2,1)} %refs_0_), channel_id=1, source_target_pairs={{0,64},{64,0},{1,65},{65,1},{2,66},{66,2},{3,67},{67,3},{4,68},{68... | collective-permute-start | bytes 1228808 | tf_op jit(solution)/shard_map/ppermute | solution.py:30
  70.7 7.2 %rotate.3 = (f32[2,128,896]{2,1,0:T(8,128)S(1)}, f32[2,128,896]{2,1,0:T(8,128)S(1)}, f32[2,128,896]{2,1,0:T(8,128)S(1)}, f32[128,896]{1,0:T(8,128)}, f32[128,896]{1,0:T(8,128)}, /*index=5*/f32[4,16,896]{2,1,0:T(8,128)S(1)}) custom-call(bf16[144,1792]{1,0:T(8,128)(2,1)S(1)} %collective-permute-done.10.g0, bf16[144,1792]{1,0:T(8,128)(2,1)S(1)} %collective-permute-done.11.g1, ...), custom_call_target="tpu_custom_call" | custom-call | flops 3439853568 | bytes 12582912 | tf_op jit(solution)/shard_map/rotate/pallas_call | solution.py:102
  79.6 6.5 %collective-permute-done.23 = f32[2,16,896]{2,1,0:T(8,128)S(1)} collective-permute-done((f32[2,16,896]{2,1,0:T(8,128)S(1)}, f32[2,16,896]{2,1,0:T(8,128)S(1)}, u32[]{:S(2)}, u32[]{:S(2)}) %collective-permute-start.23) | collective-permute-done | bytes 114720 | tf_op jit(solution)/shard_map/ppermute | solution.py:30
  86.2 5.7 %collective-permute-done.24 = f32[2,16,896]{2,1,0:T(8,128)S(1)} collective-permute-done((f32[2,16,896]{2,1,0:T(8,128)S(1)}, f32[2,16,896]{2,1,0:T(8,128)S(1)}, u32[]{:S(2)}, u32[]{:S(2)}) %collective-permute-start.24) | collective-permute-done | bytes 114720 | tf_op jit(solution)/shard_map/ppermute | solution.py:30
  91.9 3.9 %collective-permute-done.25 = f32[2,16,896]{2,1,0:T(8,128)S(1)} collective-permute-done((f32[2,16,896]{2,1,0:T(8,128)S(1)}, f32[2,16,896]{2,1,0:T(8,128)S(1)}, u32[]{:S(2)}, u32[]{:S(2)}) %collective-permute-start.25) | collective-permute-done | bytes 114720 | tf_op jit(solution)/shard_map/ppermute | solution.py:30
  99.8 7.0 %collective-permute-done.20.refs_3_ = bf16[320,640]{1,0:T(8,128)(2,1)S(1)} collective-permute-done((bf16[320,640]{1,0:T(8,128)(2,1)}, bf16[320,640]{1,0:T(8,128)(2,1)S(1)}, u32[]{:S(2)}, u32[]{:S(2)}) %collective-permute-start.20) | collective-permute-done | bytes 409632 | tf_op jit(solution)/shard_map/ppermute | solution.py:30
  119.7 7.8 %collective-permute-done.32.refs_2_ = bf16[320,640]{1,0:T(8,128)(2,1)S(1)} collective-permute-done((bf16[320,640]{1,0:T(8,128)(2,1)}, bf16[320,640]{1,0:T(8,128)(2,1)S(1)}, u32[]{:S(2)}, u32[]{:S(2)}) %collective-permute-start.32) | collective-permute-done | bytes 409632 | tf_op jit(solution)/shard_map/ppermute | solution.py:30
  130.1 3.2 %rotate_acts.1 = (f32[144,640]{1,0:T(8,128)S(1)}, f32[144,640]{1,0:T(8,128)S(1)}) custom-call(s32[8]{0:T(128)S(1)} %stack.178.order, bf16[8,288,320]{2,1,0:T(8,128)(2,1)S(1)} %constant_dynamic-update-slice_fusion.acts, bf16[320,640]{1,0:T(8,128)(2,1)} %refs_0_, bf16[320,640]{1,0:T(8,128)(2,1)} %collective-permute-done.19.refs_1_, ...), custom_call_target="tpu_custom_call" | custom-call | flops 943718400 | bytes 6291456 | tf_op jit(solution)/shard_map/rotate_acts/pallas_call | solution.py:187
  133.3 14.2 %collective-permute-start.39 = (f32[144,640]{1,0:T(8,128)S(1)}, f32[144,640]{1,0:T(8,128)S(1)}, u32[]{:S(2)}, u32[]{:S(2)}) collective-permute-start(f32[144,640]{1,0:T(8,128)S(1)} %get-tuple-element.200), channel_id=1, source_target_pairs={{0,8},{8,0},{1,9},{9,1},{2,10},{10,2},{3,11},{11,3},{4,12},{12,4},... | collective-permute-start | bytes 1105928 | tf_op jit(solution)/shard_map/ppermute | solution.py:30
  148.3 3.2 %collective-permute-start.43 = (bf16[16,896]{1,0:T(8,128)(2,1)S(1)}, bf16[16,896]{1,0:T(8,128)(2,1)S(1)}, u32[]{:S(2)}, u32[]{:S(2)}) collective-permute-start(bf16[16,896]{1,0:T(8,128)(2,1)S(1)} %fusion.14), channel_id=1, source_target_pairs={{0,3},{1,0},{2,1},{3,2},{4,7},{5,4},{6,5},{7,6},{8,11},{9,8},{10,9... | collective-permute-start | bytes 86024 | tf_op jit(solution)/shard_map/ppermute | solution.py:30
  153.6 6.8 %collective-permute-done.43 = bf16[16,896]{1,0:T(8,128)(2,1)S(1)} collective-permute-done((bf16[16,896]{1,0:T(8,128)(2,1)S(1)}, bf16[16,896]{1,0:T(8,128)(2,1)S(1)}, u32[]{:S(2)}, u32[]{:S(2)}) %collective-permute-start.43) | collective-permute-done | bytes 28704 | tf_op jit(solution)/shard_map/ppermute | solution.py:30
  160.9 7.3 %collective-permute-done.45 = bf16[16,896]{1,0:T(8,128)(2,1)S(1)} collective-permute-done((bf16[16,896]{1,0:T(8,128)(2,1)S(1)}, bf16[16,896]{1,0:T(8,128)(2,1)S(1)}, u32[]{:S(2)}, u32[]{:S(2)}) %collective-permute-start.45) | collective-permute-done | bytes 28704 | tf_op jit(solution)/shard_map/ppermute | solution.py:30
  189.3 5.7 %collective-permute-start.56 = (bf16[2,896,640]{2,1,0:T(8,128)(2,1)S(1)}, bf16[2,896,640]{2,1,0:T(8,128)(2,1)}, u32[]{:S(2)}, u32[]{:S(2)}) collective-permute-start(bf16[2,896,640]{2,1,0:T(8,128)(2,1)S(1)} %pad_maximum_fusion.refs_9_.refs_8_), channel_id=1, source_target_pairs={{0,8},{8,0},{1,9},{9,1},{2,10},{10,2},{3,11},{11,3},{4,12},{12,4},... | collective-permute-start | bytes 6881288 | tf_op jit(solution)/shard_map/ppermute | solution.py:30
  196.6 10.7 %collective-permute-done.53.refs_1_ = bf16[2,2,64,896]{3,2,1,0:T(8,128)(2,1)} collective-permute-done((bf16[2,2,64,896]{3,2,1,0:T(8,128)(2,1)S(1)}, bf16[2,2,64,896]{3,2,1,0:T(8,128)(2,1)}, u32[]{:S(2)}, u32[]{:S(2)}) %collective-permute-start.53) | collective-permute-done | bytes 458784 | tf_op jit(solution)/shard_map/ppermute | solution.py:30
  209.0 10.2 %collective-permute-done.55.refs_3_ = bf16[2,2,64,896]{3,2,1,0:T(8,128)(2,1)} collective-permute-done((bf16[2,2,64,896]{3,2,1,0:T(8,128)(2,1)S(1)}, bf16[2,2,64,896]{3,2,1,0:T(8,128)(2,1)}, u32[]{:S(2)}, u32[]{:S(2)}) %collective-permute-start.55) | collective-permute-done | bytes 458784 | tf_op jit(solution)/shard_map/ppermute | solution.py:30
  223.8 5.4 %score.2 = f32[512,2]{1,0:T(8,128)S(1)} custom-call(bf16[2,64,896]{2,1,0:T(8,128)(2,1)S(1)} %add_convert_fusion.1.refs_0_, bf16[2,64,896]{2,1,0:T(8,128)(2,1)S(1)} %collective-permute-done.36.refs_1_, bf16[2,64,896]{2,1,0:T(8,128)(2,1)S(1)} %collective-permute-done.37.refs_2_, bf16[2,64,896]{2,1,0:T(8,128)(2,1)S(1)} %copy-done.6, ...), custom_call_target="tpu_custom_call" | custom-call | flops 2264924160 | bytes 8388608 | tf_op jit(solution)/shard_map/score/pallas_call | solution.py:161
  233.1 5.5 %score.3 = f32[512,2]{1,0:T(8,128)S(1)} custom-call(bf16[2,2,64,896]{3,2,1,0:T(8,128)(2,1)S(1)} %pad_maximum_fusion.3.refs_0_, bf16[2,2,64,896]{3,2,1,0:T(8,128)(2,1)} %collective-permute-done.53.refs_1_, bf16[2,2,64,896]{3,2,1,0:T(8,128)(2,1)} %collective-permute-done.54.refs_2_, bf16[2,2,64,896]{3,2,1,0:T(8,128)(2,1)} %collective-permute-done.55.refs_3_, ...), custom_call_target="tpu_custom_call" | custom-call | flops 2264924160 | bytes 8388608 | tf_op jit(solution)/shard_map/score/pallas_call | solution.py:161
  240.7 6.3 %all-to-all-start = ((f32[128,2,128]{2,1,0:T(2,128)}), f32[128,2,128]{2,1,0:T(2,128)S(1)}, u32[]{:S(2)}, u32[]{:S(2)}) async-start(f32[128,2,128]{2,1,0:T(2,128)} %bitcast.73), calls=%async_computation | async-start | bytes 262144 | tf_op jit(solution)/shard_map/all_to_all | solution.py:367
  247.8 9.3 %all-to-all-done = f32[128,2,128]{2,1,0:T(2,128)S(1)} async-done(((f32[128,2,128]{2,1,0:T(2,128)}), f32[128,2,128]{2,1,0:T(2,128)S(1)}, u32[]{:S(2)}, u32[]{:S(2)}) %all-to-all-start) | async-done | bytes 131104 | tf_op jit(solution)/shard_map/all_to_all | solution.py:367
  (268 shorter events, 98.6 us)
Async XLA Ops:
  2.8 31.4 %collective-permute-start.4 = (bf16[1792,896]{1,0:T(8,128)(2,1)S(1)}, bf16[1792,896]{1,0:T(8,128)(2,1)}, u32[]{:S(2)}, u32[]{:S(2)}) collective-permute-start(bf16[1792,896]{1,0:T(8,128)(2,1)S(1)} %pad.21.own_basis), channel_id=1, source_target_pairs={{0,8},{8,0},{1,9},{9,1},{2,10},{10,2},{3,11},{11,3},{4,12},{12,4},... | collective-permute-start | bytes 9633800 | tf_op jit(solution)/shard_map/ppermute | solution.py:30
  14.8 19.4 %collective-permute-start.1 = (bf16[144,1792]{1,0:T(8,128)(2,1)S(1)}, bf16[144,1792]{1,0:T(8,128)(2,1)S(1)}, u32[]{:S(2)}, u32[]{:S(2)}) collective-permute-start(bf16[144,1792]{1,0:T(8,128)(2,1)S(1)} %fusion.4.g0), channel_id=1, source_target_pairs={{0,64},{64,0},{1,65},{65,1},{2,66},{66,2},{3,67},{67,3},{4,68},{68... | collective-permute-start | bytes 1548296 | tf_op jit(solution)/shard_map/ppermute | solution.py:30
  17.6 16.6 %collective-permute-start.2 = (bf16[144,1792]{1,0:T(8,128)(2,1)S(1)}, bf16[144,1792]{1,0:T(8,128)(2,1)S(1)}, u32[]{:S(2)}, u32[]{:S(2)}) collective-permute-start(bf16[144,1792]{1,0:T(8,128)(2,1)S(1)} %fusion.4.g0), channel_id=1, source_target_pairs={{0,48},{16,0},{32,16},{48,32},{1,49},{17,1},{33,17},{49,33},{2,50}... | collective-permute-start | bytes 1548296 | tf_op jit(solution)/shard_map/ppermute | solution.py:30
  20.4 13.9 %collective-permute-start.3 = (bf16[144,1792]{1,0:T(8,128)(2,1)S(1)}, bf16[144,1792]{1,0:T(8,128)(2,1)S(1)}, u32[]{:S(2)}, u32[]{:S(2)}) collective-permute-start(bf16[144,1792]{1,0:T(8,128)(2,1)S(1)} %fusion.4.g0), channel_id=1, source_target_pairs={{0,16},{16,32},{32,48},{48,0},{1,17},{17,33},{33,49},{49,1},{2,18}... | collective-permute-start | bytes 1548296 | tf_op jit(solution)/shard_map/ppermute | solution.py:30
  34.2 12.6 %collective-permute-start.10 = (bf16[144,1792]{1,0:T(8,128)(2,1)S(1)}, bf16[144,1792]{1,0:T(8,128)(2,1)S(1)}, u32[]{:S(2)}, u32[]{:S(2)}) collective-permute-start(bf16[144,1792]{1,0:T(8,128)(2,1)S(1)} %collective-permute-done.1.g1), channel_id=1, source_target_pairs={{0,48},{16,0},{32,16},{48,32},{1,49},{17,1},{33,17},{49,33},{2,50}... | collective-permute-start | bytes 1548296 | tf_op jit(solution)/shard_map/ppermute | solution.py:30
  36.5 19.3 %collective-permute-start.14 = (bf16[144,1792]{1,0:T(8,128)(2,1)S(1)}, bf16[144,1792]{1,0:T(8,128)(2,1)S(1)}, u32[]{:S(2)}, u32[]{:S(2)}) collective-permute-start(bf16[144,1792]{1,0:T(8,128)(2,1)S(1)} %collective-permute-done.2.g2), channel_id=1, source_target_pairs={{0,48},{16,0},{32,16},{48,32},{1,49},{17,1},{33,17},{49,33},{2,50}... | collective-permute-start | bytes 1548296 | tf_op jit(solution)/shard_map/ppermute | solution.py:30
  50.3 29.2 %collective-permute-start.26 = (bf16[4,288,320]{2,1,0:T(8,128)(2,1)S(1)}, bf16[4,288,320]{2,1,0:T(8,128)(2,1)S(1)}, u32[]{:S(2)}, u32[]{:S(2)}) collective-permute-start(bf16[4,288,320]{2,1,0:T(8,128)(2,1)S(1)} %pad_maximum_fusion.2), channel_id=1, source_target_pairs={{0,4},{4,0},{1,5},{5,1},{2,6},{6,2},{3,7},{7,3},{8,12},{12,8},{9,1... | collective-permute-start | bytes 2211848 | tf_op jit(solution)/shard_map/ppermute | solution.py:30
  59.6 36.2 %collective-permute-start.18 = (bf16[320,640]{1,0:T(8,128)(2,1)}, bf16[320,640]{1,0:T(8,128)(2,1)}, u32[]{:S(2)}, u32[]{:S(2)}) collective-permute-start(bf16[320,640]{1,0:T(8,128)(2,1)} %refs_0_), channel_id=1, source_target_pairs={{0,64},{64,0},{1,65},{65,1},{2,66},{66,2},{3,67},{67,3},{4,68},{68... | collective-permute-start | bytes 1228808 | tf_op jit(solution)/shard_map/ppermute | solution.py:30
  64.2 34.2 %collective-permute-start.19 = (bf16[320,640]{1,0:T(8,128)(2,1)}, bf16[320,640]{1,0:T(8,128)(2,1)}, u32[]{:S(2)}, u32[]{:S(2)}) collective-permute-start(bf16[320,640]{1,0:T(8,128)(2,1)} %refs_0_), channel_id=1, source_target_pairs={{0,48},{16,0},{32,16},{48,32},{1,49},{17,1},{33,17},{49,33},{2,50}... | collective-permute-start | bytes 1228808 | tf_op jit(solution)/shard_map/ppermute | solution.py:30
  66.1 40.6 %collective-permute-start.16 = (f32[2,128,896]{2,1,0:T(8,128)}, f32[2,128,896]{2,1,0:T(8,128)}, u32[]{:S(2)}, u32[]{:S(2)}) collective-permute-start(f32[2,128,896]{2,1,0:T(8,128)} %fusion.8), channel_id=1, source_target_pairs={{0,1},{1,2},{2,3},{3,0},{4,5},{5,6},{6,7},{7,4},{8,9},{9,10},{10,1... | collective-permute-start | bytes 2752520 | tf_op jit(solution)/shard_map/ppermute | solution.py:30
  68.1 38.7 %collective-permute-start.17 = (f32[2,128,896]{2,1,0:T(8,128)}, f32[2,128,896]{2,1,0:T(8,128)}, u32[]{:S(2)}, u32[]{:S(2)}) collective-permute-start(f32[2,128,896]{2,1,0:T(8,128)} %fusion.7), channel_id=1, source_target_pairs={{0,3},{1,0},{2,1},{3,2},{4,7},{5,4},{6,5},{7,6},{8,11},{9,8},{10,9... | collective-permute-start | bytes 2752520 | tf_op jit(solution)/shard_map/ppermute | solution.py:30
  106.9 12.4 %collective-permute-start.31 = (bf16[320,640]{1,0:T(8,128)(2,1)}, bf16[320,640]{1,0:T(8,128)(2,1)S(1)}, u32[]{:S(2)}, u32[]{:S(2)}) collective-permute-start(bf16[320,640]{1,0:T(8,128)(2,1)} %collective-permute-done.18.refs_4_), channel_id=1, source_target_pairs={{0,16},{16,32},{32,48},{48,0},{1,17},{17,33},{33,49},{49,1},{2,18}... | collective-permute-start | bytes 1228808 | tf_op jit(solution)/shard_map/ppermute | solution.py:30
  110.3 19.8 %collective-permute-start.27 = (f32[2,128,896]{2,1,0:T(8,128)}, f32[2,128,896]{2,1,0:T(8,128)S(1)}, u32[]{:S(2)}, u32[]{:S(2)}) collective-permute-start(f32[2,128,896]{2,1,0:T(8,128)} %fusion.6), channel_id=1, source_target_pairs={{0,1},{1,2},{2,3},{3,0},{4,5},{5,6},{6,7},{7,4},{8,9},{9,10},{10,1... | collective-permute-start | bytes 2752520 | tf_op jit(solution)/shard_map/ppermute | solution.py:30
  111.5 18.6 %collective-permute-start.28 = (f32[2,128,896]{2,1,0:T(8,128)S(1)}, f32[2,128,896]{2,1,0:T(8,128)S(1)}, u32[]{:S(2)}, u32[]{:S(2)}) collective-permute-start(f32[2,128,896]{2,1,0:T(8,128)S(1)} %fusion.5), channel_id=1, source_target_pairs={{0,3},{1,0},{2,1},{3,2},{4,7},{5,4},{6,5},{7,6},{8,11},{9,8},{10,9... | collective-permute-start | bytes 2752520 | tf_op jit(solution)/shard_map/ppermute | solution.py:30
  133.3 18.4 %collective-permute-start.39 = (f32[144,640]{1,0:T(8,128)S(1)}, f32[144,640]{1,0:T(8,128)S(1)}, u32[]{:S(2)}, u32[]{:S(2)}) collective-permute-start(f32[144,640]{1,0:T(8,128)S(1)} %get-tuple-element.200), channel_id=1, source_target_pairs={{0,8},{8,0},{1,9},{9,1},{2,10},{10,2},{3,11},{11,3},{4,12},{12,4},... | collective-permute-start | bytes 1105928 | tf_op jit(solution)/shard_map/ppermute | solution.py:30
  147.5 22.4 %collective-permute-start.36 = (bf16[2,64,896]{2,1,0:T(8,128)(2,1)S(1)}, bf16[2,64,896]{2,1,0:T(8,128)(2,1)S(1)}, u32[]{:S(2)}, u32[]{:S(2)}) collective-permute-start(bf16[2,64,896]{2,1,0:T(8,128)(2,1)S(1)} %add_convert_fusion.1.refs_0_), channel_id=1, source_target_pairs={{0,3},{1,0},{2,1},{3,2},{4,7},{5,4},{6,5},{7,6},{8,11},{9,8},{10,9... | collective-permute-start | bytes 688136 | tf_op jit(solution)/shard_map/ppermute | solution.py:30
  148.3 21.7 %collective-permute-start.37 = (bf16[2,64,896]{2,1,0:T(8,128)(2,1)S(1)}, bf16[2,64,896]{2,1,0:T(8,128)(2,1)S(1)}, u32[]{:S(2)}, u32[]{:S(2)}) collective-permute-start(bf16[2,64,896]{2,1,0:T(8,128)(2,1)S(1)} %add_convert_fusion.1.refs_0_), channel_id=1, source_target_pairs={{0,2},{1,3},{2,0},{3,1},{4,6},{5,7},{6,4},{7,5},{8,10},{9,11},{10,... | collective-permute-start | bytes 688136 | tf_op jit(solution)/shard_map/ppermute | solution.py:30
  151.7 20.4 %collective-permute-start.35 = (f32[2,64,896]{2,1,0:T(8,128)S(1)}, f32[2,64,896]{2,1,0:T(8,128)S(1)}, u32[]{:S(2)}, u32[]{:S(2)}) collective-permute-start(f32[2,64,896]{2,1,0:T(8,128)S(1)} %get-tuple-element.192), channel_id=1, source_target_pairs={{0,4},{4,0},{1,5},{5,1},{2,6},{6,2},{3,7},{7,3},{8,12},{12,8},{9,1... | collective-permute-start | bytes 1376264 | tf_op jit(solution)/shard_map/ppermute | solution.py:30
  189.3 29.8 %collective-permute-start.56 = (bf16[2,896,640]{2,1,0:T(8,128)(2,1)S(1)}, bf16[2,896,640]{2,1,0:T(8,128)(2,1)}, u32[]{:S(2)}, u32[]{:S(2)}) collective-permute-start(bf16[2,896,640]{2,1,0:T(8,128)(2,1)S(1)} %pad_maximum_fusion.refs_9_.refs_8_), channel_id=1, source_target_pairs={{0,8},{8,0},{1,9},{9,1},{2,10},{10,2},{3,11},{11,3},{4,12},{12,4},... | collective-permute-start | bytes 6881288 | tf_op jit(solution)/shard_map/ppermute | solution.py:30
  195.0 24.2 %collective-permute-start.52 = (bf16[4,2,64,896]{3,2,1,0:T(8,128)(2,1)}, bf16[4,2,64,896]{3,2,1,0:T(8,128)(2,1)}, u32[]{:S(2)}, u32[]{:S(2)}) collective-permute-start(bf16[4,2,64,896]{3,2,1,0:T(8,128)(2,1)} %pad_maximum_fusion.1), channel_id=1, source_target_pairs={{0,4},{4,0},{1,5},{5,1},{2,6},{6,2},{3,7},{7,3},{8,12},{12,8},{9,1... | collective-permute-start | bytes 2752520 | tf_op jit(solution)/shard_map/ppermute | solution.py:30
  195.1 12.3 %collective-permute-start.53 = (bf16[2,2,64,896]{3,2,1,0:T(8,128)(2,1)S(1)}, bf16[2,2,64,896]{3,2,1,0:T(8,128)(2,1)}, u32[]{:S(2)}, u32[]{:S(2)}) collective-permute-start(bf16[2,2,64,896]{3,2,1,0:T(8,128)(2,1)S(1)} %pad_maximum_fusion.3.refs_0_), channel_id=1, source_target_pairs={{0,3},{1,0},{2,1},{3,2},{4,7},{5,4},{6,5},{7,6},{8,11},{9,8},{10,9... | collective-permute-start | bytes 1376264 | tf_op jit(solution)/shard_map/ppermute | solution.py:30
  195.1 13.8 %collective-permute-start.54 = (bf16[2,2,64,896]{3,2,1,0:T(8,128)(2,1)S(1)}, bf16[2,2,64,896]{3,2,1,0:T(8,128)(2,1)}, u32[]{:S(2)}, u32[]{:S(2)}) collective-permute-start(bf16[2,2,64,896]{3,2,1,0:T(8,128)(2,1)S(1)} %pad_maximum_fusion.3.refs_0_), channel_id=1, source_target_pairs={{0,2},{1,3},{2,0},{3,1},{4,6},{5,7},{6,4},{7,5},{8,10},{9,11},{10,... | collective-permute-start | bytes 1376264 | tf_op jit(solution)/shard_map/ppermute | solution.py:30
  195.6 23.5 %collective-permute-start.55 = (bf16[2,2,64,896]{3,2,1,0:T(8,128)(2,1)S(1)}, bf16[2,2,64,896]{3,2,1,0:T(8,128)(2,1)}, u32[]{:S(2)}, u32[]{:S(2)}) collective-permute-start(bf16[2,2,64,896]{3,2,1,0:T(8,128)(2,1)S(1)} %pad_maximum_fusion.3.refs_0_), channel_id=1, source_target_pairs={{0,1},{1,2},{2,3},{3,0},{4,5},{5,6},{6,7},{7,4},{8,9},{9,10},{10,1... | collective-permute-start | bytes 1376264 | tf_op jit(solution)/shard_map/ppermute | solution.py:30
  240.7 16.3 %all-to-all-start = ((f32[128,2,128]{2,1,0:T(2,128)}), f32[128,2,128]{2,1,0:T(2,128)S(1)}, u32[]{:S(2)}, u32[]{:S(2)}) async-start(f32[128,2,128]{2,1,0:T(2,128)} %bitcast.73), calls=%async_computation | async-start | bytes 262144 | tf_op jit(solution)/shard_map/all_to_all | solution.py:367
  (77 other events, 706.2 us)

commit v4 on v3

--- a/solution.py
+++ b/solution.py
@@ -138,13 +138,17 @@
 
 def score_kernel(*refs):
     blocks, acts, (own_precond, sib_precond, out) = refs[:-7], refs[-7:-3], refs[-3:]
-    if len(blocks) == 5:
-        place = [b for b in blocks[:4]] + [blocks[4].at[i] for i in range(4)]
+    if len(blocks) == 2:
+        place = [b.at[i] for b in blocks for i in range(4)]
     else:
         place = [b.at[dx] for dx in range(2) for b in blocks]
     own = jnp.concatenate([b[0] for b in place], axis=0)
     sib = jnp.concatenate([b[1] for b in place], axis=0)
-    acts = [x[...].astype(jnp.float32) for x in acts]
+    if len(blocks) == 2:
+        acts = (acts[0][0], acts[0][1], acts[1][0], acts[3][0])
+    else:
+        acts = (acts[1][1], acts[3][1], acts[2][0], acts[2][1])
+    acts = [x.astype(jnp.float32) for x in acts]
     wide = []
     for dx in range(2):
         for dz in range(4):
@@ -250,9 +254,6 @@
     g[1, 3] = take(g[1, 0], "y", -1)
     near_1, up_1, down_1, far_own, far_sib, query_1 = rotate(
         [g[c] for c in groups[0]], own_basis, sib_basis
-    )
-    g[1, 1], g[1, 3], near_1, up_1, down_1, far_own, far_sib, query_1 = sync(
-        (g[1, 1], g[1, 3], near_1, up_1, down_1, far_own, far_sib, query_1)
     )
 
     far_own, far_sib = take(far_own, "z", -1), take(far_sib, "z", 1)
@@ -306,34 +307,25 @@
     rot_acts = jnp.concatenate(
         [own_rows_first(rot_acts[:count], x_lo, z), rot_acts[count:]], axis=0
     )
-    r = {(0, 0): rot_acts}
-    r[1, 0] = take(r[0, 0], "x_hi", 1)
-    r[0, 1] = take(r[0, 0], "y", 1)
-    r[0, 3] = take(r[0, 0], "y", -1)
+    pair = jnp.stack([rot_acts, take(rot_acts, "x_hi", 1)])
     query_own = (pieces[0] + query_x).astype(jnp.bfloat16)
     query_near = [take(query_own, "z", d) for d in (1, 2, 3)]
-    kept_2, other_2, near_1, r[1, 0], r[0, 1], r[0, 3], query_near = sync(
-        (kept_2, other_2, near_1, r[1, 0], r[0, 1], r[0, 3], query_near)
-    )
 
     mean_2 = (kept_2 + other_2).astype(jnp.bfloat16)
     pair_2 = take(mean_2, "x_lo", 1)
     query_near = jnp.stack([query_own] + query_near)
     query_far = take(query_near, "x_lo", 1)
-    r[1, 1] = take(r[1, 0], "y", 1)
-    r[1, 3] = take(r[1, 0], "y", -1)
-    r[0, 2] = take(r[0, 1], "y", 1)
-    r[1, 2] = take(r[1, 3], "y", -1)
+    pairs = [pair, take(pair, "y", 1), take(pair, "y", 2), take(pair, "y", -1)]
     near_1 = [mean_1] + near_1
     near_1_all = jnp.stack(near_1)
-    pair_2, query_far, r[1, 1], r[1, 3], r[0, 2], r[1, 2], near_1_all = sync(
-        (pair_2, query_far, r[1, 1], r[1, 3], r[0, 2], r[1, 2], near_1_all)
+    pair_2, query_far, pairs, near_1_all = sync(
+        (pair_2, query_far, pairs, near_1_all)
     )
 
     far_1 = take(near_1_all, "x_lo", 1)
     pair_2 = jnp.stack([mean_2, pair_2])
     pairs_2 = [pair_2] + [take(pair_2, "z", d) for d in (1, 2, 3)]
-    query_acts_all = jnp.concatenate([r[c][count:] for c in chips], axis=0)
+    query_acts_all = jnp.concatenate([pairs[d][h, count:] for h, d in chips], axis=0)
     query_acts_all = own_rows_first(query_acts_all, x_lo, z).reshape(4, 2, ROWS, -1)
     query_len = 4 * ROWS
     divisor = query_len * (pad_to(eigvals, wide, eigvals.shape[1], value=1.0) + damping)
@@ -347,14 +339,12 @@
         precond.append((numerator / divisor).astype(jnp.bfloat16))
     own_precond = jnp.stack(precond)
     sib_precond = take(own_precond, "core", 1)
-    far_1, pairs_2, sib_precond = sync((far_1, pairs_2, sib_precond))
-    shards = r
-    rotated = (near_1 + [far_1], pairs_2)
 
     scores = {}
-    for group, blocks in zip(groups, rotated):
-        result = score(blocks, [shards[c] for c in group], own_precond, sib_precond)
-        scores.update((c, result[:, :, s]) for s, c in enumerate(group))
+    result = score([near_1_all, far_1], pairs, own_precond, sib_precond)
+    pairs_2, result = sync((pairs_2, result))
+    for group, part in zip(groups, (result, score(pairs_2, pairs, own_precond, sib_precond))):
+        scores.update((c, part[:, :, s]) for s, c in enumerate(group))
     stacked = jnp.stack([scores[c] for c in chips]).reshape(2, 4, 2, 4, ROWS, QUERIES)
     stacked = stacked.transpose(5, 0, 1, 2, 3, 4)
     stacked = jnp.where(x_lo != x_hi, stacked[::-1], stacked)

time: 259 us -> 251 us (0.969)
  starting transfers between devices: 82.2 us -> 74.4 us
    ppermute x57 -> x54, starting transfers between devices: 75.8 us -> 69.5 us  [take(): lax.ppermute(x, axis, [(i, (i - step) % count) for i in range(count)])]
    unnamed x112 -> x96, local copies, waits for them, and re-layouts: 14.2 us -> 12.6 us
    ppermute x57 -> x54, waiting for transfers between devices: 101 us -> 102 us  [take(): lax.ppermute(x, axis, [(i, (i - step) % count) for i in range(count)])]
  transfers between devices with their start and end apart: 58 -> 55, of which waited for: 29 -> 20; matrix products, arithmetic and copies ran while one was open for 5% -> 5% of each run, Pallas kernels for 7% -> 9%
where the time goes in v4:
time: 251 us; the launch traced here: 250 us
  waiting for transfers between devices  111 us (44%)
  starting transfers between devices  74.4 us (30%)
  Pallas kernels  33 us (13%)
  local copies, waits for them, and re-layouts  17.2 us (7%)
  other arithmetic  11.2 us (4%)
    ppermute x54, waiting for transfers between devices, take(): lax.ppermute(x, axis, [(i, (i - step) % count) for i in range(count)])  102 us
    ppermute x54, starting transfers between devices, take(): lax.ppermute(x, axis, [(i, (i - step) % count) for i in range(count)])  69.5 us
    pallas_call x2, Pallas kernels, rotate(): pl.pallas_call(rotate_kernel, out_shape=(pair, pair, pair, single, single...  14.7 us
    unnamed x96, local copies, waits for them, and re-layouts  12.6 us
    pallas_call x2, Pallas kernels, score(): pl.pallas_call(score_kernel, out_shape=jax.ShapeDtypeStruct((GROUP * SEQL...  11 us
    all_to_all x1, waiting for transfers between devices, per_device(): lax.all_to_all(spread.reshape(128, QUERIES, SEQLEN), AXES, 0, 0, tiled=True)  9.28 us
  transfers between devices with their start and end apart: 55, of which 20 were waited for; matrix products, arithmetic and copies ran while one was open for 5% of the time, Pallas kernels for 9%

profile of v4, /device:TPU:1, one launch (start us, length us, event | category | flops | bytes accessed | tf_op | source)
XLA Modules:
  0.0 250.5 jit_solution(14102500651072695410)
XLA Ops:
  10.9 3.9 %collective-permute-start.7 = (bf16[288,320]{1,0:T(8,128)(2,1)S(1)}, bf16[288,320]{1,0:T(8,128)(2,1)S(1)}, u32[]{:S(2)}, u32[]{:S(2)}) collective-permute-start(bf16[288,320]{1,0:T(8,128)(2,1)S(1)} %get-tuple-element.196), channel_id=1, source_target_pairs={{0,3},{1,0},{2,1},{3,2},{4,7},{5,4},{6,5},{7,6},{8,11},{9,8},{10,9... | collective-permute-start | bytes 552968 | tf_op jit(solution)/shard_map/ppermute | solution.py:30
  21.5 6.4 %collective-permute-done.8 = bf16[288,320]{1,0:T(8,128)(2,1)S(1)} collective-permute-done((bf16[288,320]{1,0:T(8,128)(2,1)S(1)}, bf16[288,320]{1,0:T(8,128)(2,1)S(1)}, u32[]{:S(2)}, u32[]{:S(2)}) %collective-permute-start.8) | collective-permute-done | bytes 184352 | tf_op jit(solution)/shard_map/ppermute | solution.py:30
  28.3 5.9 %collective-permute-done.9 = bf16[288,320]{1,0:T(8,128)(2,1)S(1)} collective-permute-done((bf16[288,320]{1,0:T(8,128)(2,1)S(1)}, bf16[288,320]{1,0:T(8,128)(2,1)S(1)}, u32[]{:S(2)}, u32[]{:S(2)}) %collective-permute-start.9) | collective-permute-done | bytes 184352 | tf_op jit(solution)/shard_map/ppermute | solution.py:30
  38.0 7.6 %rotate.2 = (f32[2,128,896]{2,1,0:T(8,128)S(1)}, f32[2,128,896]{2,1,0:T(8,128)}, f32[2,128,896]{2,1,0:T(8,128)}, f32[128,896]{1,0:T(8,128)S(1)}, f32[128,896]{1,0:T(8,128)S(1)}, /*index=5*/f32[4,16,896]{2,1,0:T(8,128)S(1)}) custom-call(bf16[144,1792]{1,0:T(8,128)(2,1)S(1)} %fusion.4.g0, bf16[144,1792]{1,0:T(8,128)(2,1)S(1)} %collective-permute-done.1.g1, ...), custom_call_target="tpu_custom_call" | custom-call | flops 3439853568 | bytes 12582912 | tf_op jit(solution)/shard_map/rotate/pallas_call | solution.py:102
  49.0 5.7 %collective-permute-done.10 = f32[128,896]{1,0:T(8,128)S(1)} collective-permute-done((f32[128,896]{1,0:T(8,128)S(1)}, f32[128,896]{1,0:T(8,128)S(1)}, u32[]{:S(2)}, u32[]{:S(2)}) %collective-permute-start.10) | collective-permute-done | bytes 458784 | tf_op jit(solution)/shard_map/ppermute | solution.py:30
  58.1 4.0 %collective-permute-start.17 = (bf16[320,640]{1,0:T(8,128)(2,1)}, bf16[320,640]{1,0:T(8,128)(2,1)}, u32[]{:S(2)}, u32[]{:S(2)}) collective-permute-start(bf16[320,640]{1,0:T(8,128)(2,1)} %refs_0_), channel_id=1, source_target_pairs={{0,64},{64,0},{1,65},{65,1},{2,66},{66,2},{3,67},{67,3},{4,68},{68... | collective-permute-start | bytes 1228808 | tf_op jit(solution)/shard_map/ppermute | solution.py:30
  69.2 7.1 %rotate.3 = (f32[2,128,896]{2,1,0:T(8,128)S(1)}, f32[2,128,896]{2,1,0:T(8,128)S(1)}, f32[2,128,896]{2,1,0:T(8,128)S(1)}, f32[128,896]{1,0:T(8,128)}, f32[128,896]{1,0:T(8,128)}, /*index=5*/f32[4,16,896]{2,1,0:T(8,128)S(1)}) custom-call(bf16[144,1792]{1,0:T(8,128)(2,1)S(1)} %collective-permute-done.20.g0, bf16[144,1792]{1,0:T(8,128)(2,1)S(1)} %collective-permute-done.13.g1, ...), custom_call_target="tpu_custom_call" | custom-call | flops 3439853568 | bytes 12582912 | tf_op jit(solution)/shard_map/rotate/pallas_call | solution.py:102
  78.1 7.9 %collective-permute-done.23 = f32[2,16,896]{2,1,0:T(8,128)S(1)} collective-permute-done((f32[2,16,896]{2,1,0:T(8,128)S(1)}, f32[2,16,896]{2,1,0:T(8,128)S(1)}, u32[]{:S(2)}, u32[]{:S(2)}) %collective-permute-start.23) | collective-permute-done | bytes 114720 | tf_op jit(solution)/shard_map/ppermute | solution.py:30
  86.0 5.3 %collective-permute-done.24 = f32[2,16,896]{2,1,0:T(8,128)S(1)} collective-permute-done((f32[2,16,896]{2,1,0:T(8,128)S(1)}, f32[2,16,896]{2,1,0:T(8,128)S(1)}, u32[]{:S(2)}, u32[]{:S(2)}) %collective-permute-start.24) | collective-permute-done | bytes 114720 | tf_op jit(solution)/shard_map/ppermute | solution.py:30
  91.6 4.4 %collective-permute-done.25 = f32[2,16,896]{2,1,0:T(8,128)S(1)} collective-permute-done((f32[2,16,896]{2,1,0:T(8,128)S(1)}, f32[2,16,896]{2,1,0:T(8,128)S(1)}, u32[]{:S(2)}, u32[]{:S(2)}) %collective-permute-start.25) | collective-permute-done | bytes 114720 | tf_op jit(solution)/shard_map/ppermute | solution.py:30
  99.0 8.0 %collective-permute-done.19.refs_3_ = bf16[320,640]{1,0:T(8,128)(2,1)S(1)} collective-permute-done((bf16[320,640]{1,0:T(8,128)(2,1)}, bf16[320,640]{1,0:T(8,128)(2,1)S(1)}, u32[]{:S(2)}, u32[]{:S(2)}) %collective-permute-start.19) | collective-permute-done | bytes 409632 | tf_op jit(solution)/shard_map/ppermute | solution.py:30
  120.3 6.8 %collective-permute-done.32.refs_2_ = bf16[320,640]{1,0:T(8,128)(2,1)S(1)} collective-permute-done((bf16[320,640]{1,0:T(8,128)(2,1)}, bf16[320,640]{1,0:T(8,128)(2,1)S(1)}, u32[]{:S(2)}, u32[]{:S(2)}) %collective-permute-start.32) | collective-permute-done | bytes 409632 | tf_op jit(solution)/shard_map/ppermute | solution.py:30
  129.7 3.2 %rotate_acts.1 = (f32[144,640]{1,0:T(8,128)S(1)}, f32[144,640]{1,0:T(8,128)S(1)}) custom-call(s32[8]{0:T(128)S(1)} %stack.193.order, bf16[8,288,320]{2,1,0:T(8,128)(2,1)S(1)} %constant_dynamic-update-slice_fusion.acts, bf16[320,640]{1,0:T(8,128)(2,1)} %refs_0_, bf16[320,640]{1,0:T(8,128)(2,1)} %collective-permute-done.18.refs_1_, ...), custom_call_target="tpu_custom_call" | custom-call | flops 943718400 | bytes 6291456 | tf_op jit(solution)/shard_map/rotate_acts/pallas_call | solution.py:191
  132.9 14.8 %collective-permute-start.41 = (f32[144,640]{1,0:T(8,128)S(1)}, f32[144,640]{1,0:T(8,128)S(1)}, u32[]{:S(2)}, u32[]{:S(2)}) collective-permute-start(f32[144,640]{1,0:T(8,128)S(1)} %get-tuple-element.171), channel_id=1, source_target_pairs={{0,8},{8,0},{1,9},{9,1},{2,10},{10,2},{3,11},{11,3},{4,12},{12,4},... | collective-permute-start | bytes 1105928 | tf_op jit(solution)/shard_map/ppermute | solution.py:30
  154.5 10.0 %collective-permute-done.42 = bf16[144,640]{1,0:T(8,128)(2,1)S(1)} collective-permute-done((bf16[144,640]{1,0:T(8,128)(2,1)S(1)}, bf16[144,640]{1,0:T(8,128)(2,1)S(1)}, u32[]{:S(2)}, u32[]{:S(2)}) %collective-permute-start.42) | collective-permute-done | bytes 184352 | tf_op jit(solution)/shard_map/ppermute | solution.py:30
  165.2 3.3 %collective-permute-start.46 = (bf16[2,64,896]{2,1,0:T(8,128)(2,1)S(1)}, bf16[2,64,896]{2,1,0:T(8,128)(2,1)S(1)}, u32[]{:S(2)}, u32[]{:S(2)}) collective-permute-start(bf16[2,64,896]{2,1,0:T(8,128)(2,1)S(1)} %add_convert_fusion), channel_id=1, source_target_pairs={{0,3},{1,0},{2,1},{3,2},{4,7},{5,4},{6,5},{7,6},{8,11},{9,8},{10,9... | collective-permute-start | bytes 688136 | tf_op jit(solution)/shard_map/ppermute | solution.py:30
  173.3 3.2 %collective-permute-done.46 = bf16[2,64,896]{2,1,0:T(8,128)(2,1)S(1)} collective-permute-done((bf16[2,64,896]{2,1,0:T(8,128)(2,1)S(1)}, bf16[2,64,896]{2,1,0:T(8,128)(2,1)S(1)}, u32[]{:S(2)}, u32[]{:S(2)}) %collective-permute-start.46) | collective-permute-done | bytes 229408 | tf_op jit(solution)/shard_map/ppermute | solution.py:30
  177.1 4.6 %collective-permute-done.40 = bf16[4,16,896]{2,1,0:T(8,128)(2,1)S(1)} collective-permute-done((bf16[4,16,896]{2,1,0:T(8,128)(2,1)S(1)}, bf16[4,16,896]{2,1,0:T(8,128)(2,1)S(1)}, u32[]{:S(2)}, u32[]{:S(2)}) %collective-permute-start.40) | collective-permute-done | bytes 114720 | tf_op jit(solution)/shard_map/ppermute | solution.py:30
  181.8 6.7 %collective-permute-done.45.refs_5_.refs_7_ = bf16[2,144,640]{2,1,0:T(8,128)(2,1)S(1)} collective-permute-done((bf16[2,144,640]{2,1,0:T(8,128)(2,1)S(1)}, bf16[2,144,640]{2,1,0:T(8,128)(2,1)S(1)}, u32[]{:S(2)}, u32[]{:S(2)}) %collective-permute-start.45) | collective-permute-done | bytes 368672 | tf_op jit(solution)/shard_map/ppermute | solution.py:30
  194.0 19.1 %collective-permute-done.52.refs_1_ = bf16[4,2,64,896]{3,2,1,0:T(8,128)(2,1)} collective-permute-done((bf16[4,2,64,896]{3,2,1,0:T(8,128)(2,1)S(1)}, bf16[4,2,64,896]{3,2,1,0:T(8,128)(2,1)}, u32[]{:S(2)}, u32[]{:S(2)}) %collective-permute-start.52) | collective-permute-done | bytes 917536 | tf_op jit(solution)/shard_map/ppermute | solution.py:30
  217.0 5.4 %score.2 = f32[512,2]{1,0:T(8,128)S(1)} custom-call(bf16[4,2,64,896]{3,2,1,0:T(8,128)(2,1)S(1)} %pad_maximum_fusion.1.refs_0_, bf16[4,2,64,896]{3,2,1,0:T(8,128)(2,1)} %collective-permute-done.52.refs_1_, bf16[2,144,640]{2,1,0:T(8,128)(2,1)S(1)} %copy-done.6, bf16[2,144,640]{2,1,0:T(8,128)(2,1)S(1)} %copy-done.12, bf16[2,144,640]{2,1,0:T(8,128)(2,1)S(1)} %copy-done.15, ...), custom_call_target="tpu_custom_call" | custom-call | flops 2264924160 | bytes 8388608 | tf_op jit(solution)/shard_map/score/pallas_call | solution.py:165
  226.7 5.6 %score.3 = f32[512,2]{1,0:T(8,128)S(1)} custom-call(bf16[2,2,64,896]{3,2,1,0:T(8,128)(2,1)} %pad_maximum_fusion.3.refs_0_, bf16[2,2,64,896]{3,2,1,0:T(8,128)(2,1)} %collective-permute-done.49.refs_1_, bf16[2,2,64,896]{3,2,1,0:T(8,128)(2,1)} %collective-permute-done.50.refs_2_, bf16[2,2,64,896]{3,2,1,0:T(8,128)(2,1)} %collective-permute-done.51.refs_3_, ...), custom_call_target="tpu_custom_call" | custom-call | flops 2264924160 | bytes 8388608 | tf_op jit(solution)/shard_map/score/pallas_call | solution.py:165
  234.2 4.9 %all-to-all-start = ((f32[128,2,128]{2,1,0:T(2,128)}), f32[128,2,128]{2,1,0:T(2,128)S(1)}, u32[]{:S(2)}, u32[]{:S(2)}) async-start(f32[128,2,128]{2,1,0:T(2,128)} %bitcast.83), calls=%async_computation | async-start | bytes 262144 | tf_op jit(solution)/shard_map/all_to_all | solution.py:357
  239.8 9.3 %all-to-all-done = f32[128,2,128]{2,1,0:T(2,128)S(1)} async-done(((f32[128,2,128]{2,1,0:T(2,128)}), f32[128,2,128]{2,1,0:T(2,128)S(1)}, u32[]{:S(2)}, u32[]{:S(2)}) %all-to-all-start) | async-done | bytes 131104 | tf_op jit(solution)/shard_map/all_to_all | solution.py:357
  (249 shorter events, 85.2 us)
Async XLA Ops:
  2.8 31.4 %collective-permute-start.4 = (bf16[1792,896]{1,0:T(8,128)(2,1)S(1)}, bf16[1792,896]{1,0:T(8,128)(2,1)}, u32[]{:S(2)}, u32[]{:S(2)}) collective-permute-start(bf16[1792,896]{1,0:T(8,128)(2,1)S(1)} %pad.21.own_basis), channel_id=1, source_target_pairs={{0,8},{8,0},{1,9},{9,1},{2,10},{10,2},{3,11},{11,3},{4,12},{12,4},... | collective-permute-start | bytes 9633800 | tf_op jit(solution)/shard_map/ppermute | solution.py:30
  14.8 19.4 %collective-permute-start.1 = (bf16[144,1792]{1,0:T(8,128)(2,1)S(1)}, bf16[144,1792]{1,0:T(8,128)(2,1)S(1)}, u32[]{:S(2)}, u32[]{:S(2)}) collective-permute-start(bf16[144,1792]{1,0:T(8,128)(2,1)S(1)} %fusion.4.g0), channel_id=1, source_target_pairs={{0,64},{64,0},{1,65},{65,1},{2,66},{66,2},{3,67},{67,3},{4,68},{68... | collective-permute-start | bytes 1548296 | tf_op jit(solution)/shard_map/ppermute | solution.py:30
  17.6 16.6 %collective-permute-start.2 = (bf16[144,1792]{1,0:T(8,128)(2,1)S(1)}, bf16[144,1792]{1,0:T(8,128)(2,1)S(1)}, u32[]{:S(2)}, u32[]{:S(2)}) collective-permute-start(bf16[144,1792]{1,0:T(8,128)(2,1)S(1)} %fusion.4.g0), channel_id=1, source_target_pairs={{0,48},{16,0},{32,16},{48,32},{1,49},{17,1},{33,17},{49,33},{2,50}... | collective-permute-start | bytes 1548296 | tf_op jit(solution)/shard_map/ppermute | solution.py:30
  34.2 14.0 %collective-permute-start.13 = (bf16[144,1792]{1,0:T(8,128)(2,1)S(1)}, bf16[144,1792]{1,0:T(8,128)(2,1)S(1)}, u32[]{:S(2)}, u32[]{:S(2)}) collective-permute-start(bf16[144,1792]{1,0:T(8,128)(2,1)S(1)} %collective-permute-done.1.g1), channel_id=1, source_target_pairs={{0,16},{16,32},{32,48},{48,0},{1,17},{17,33},{33,49},{49,1},{2,18}... | collective-permute-start | bytes 1548296 | tf_op jit(solution)/shard_map/ppermute | solution.py:30
  35.6 30.9 %collective-permute-start.20 = (bf16[144,1792]{1,0:T(8,128)(2,1)S(1)}, bf16[144,1792]{1,0:T(8,128)(2,1)S(1)}, u32[]{:S(2)}, u32[]{:S(2)}) collective-permute-start(bf16[144,1792]{1,0:T(8,128)(2,1)S(1)} %collective-permute-done.1.g1), channel_id=1, source_target_pairs={{0,48},{16,0},{32,16},{48,32},{1,49},{17,1},{33,17},{49,33},{2,50}... | collective-permute-start | bytes 1548296 | tf_op jit(solution)/shard_map/ppermute | solution.py:30
  37.0 20.2 %collective-permute-start.12 = (bf16[144,1792]{1,0:T(8,128)(2,1)S(1)}, bf16[144,1792]{1,0:T(8,128)(2,1)S(1)}, u32[]{:S(2)}, u32[]{:S(2)}) collective-permute-start(bf16[144,1792]{1,0:T(8,128)(2,1)S(1)} %collective-permute-done.2.g2), channel_id=1, source_target_pairs={{0,48},{16,0},{32,16},{48,32},{1,49},{17,1},{33,17},{49,33},{2,50}... | collective-permute-start | bytes 1548296 | tf_op jit(solution)/shard_map/ppermute | solution.py:30
  54.7 23.2 %collective-permute-start.26 = (bf16[4,288,320]{2,1,0:T(8,128)(2,1)S(1)}, bf16[4,288,320]{2,1,0:T(8,128)(2,1)S(1)}, u32[]{:S(2)}, u32[]{:S(2)}) collective-permute-start(bf16[4,288,320]{2,1,0:T(8,128)(2,1)S(1)} %pad_maximum_fusion.2), channel_id=1, source_target_pairs={{0,4},{4,0},{1,5},{5,1},{2,6},{6,2},{3,7},{7,3},{8,12},{12,8},{9,1... | collective-permute-start | bytes 2211848 | tf_op jit(solution)/shard_map/ppermute | solution.py:30
  58.1 37.9 %collective-permute-start.17 = (bf16[320,640]{1,0:T(8,128)(2,1)}, bf16[320,640]{1,0:T(8,128)(2,1)}, u32[]{:S(2)}, u32[]{:S(2)}) collective-permute-start(bf16[320,640]{1,0:T(8,128)(2,1)} %refs_0_), channel_id=1, source_target_pairs={{0,64},{64,0},{1,65},{65,1},{2,66},{66,2},{3,67},{67,3},{4,68},{68... | collective-permute-start | bytes 1228808 | tf_op jit(solution)/shard_map/ppermute | solution.py:30
  62.1 36.6 %collective-permute-start.18 = (bf16[320,640]{1,0:T(8,128)(2,1)}, bf16[320,640]{1,0:T(8,128)(2,1)}, u32[]{:S(2)}, u32[]{:S(2)}) collective-permute-start(bf16[320,640]{1,0:T(8,128)(2,1)} %refs_0_), channel_id=1, source_target_pairs={{0,48},{16,0},{32,16},{48,32},{1,49},{17,1},{33,17},{49,33},{2,50}... | collective-permute-start | bytes 1228808 | tf_op jit(solution)/shard_map/ppermute | solution.py:30
  64.6 42.4 %collective-permute-start.15 = (f32[2,128,896]{2,1,0:T(8,128)}, f32[2,128,896]{2,1,0:T(8,128)}, u32[]{:S(2)}, u32[]{:S(2)}) collective-permute-start(f32[2,128,896]{2,1,0:T(8,128)} %fusion.8), channel_id=1, source_target_pairs={{0,1},{1,2},{2,3},{3,0},{4,5},{5,6},{6,7},{7,4},{8,9},{9,10},{10,1... | collective-permute-start | bytes 2752520 | tf_op jit(solution)/shard_map/ppermute | solution.py:30
  66.5 40.5 %collective-permute-start.16 = (f32[2,128,896]{2,1,0:T(8,128)}, f32[2,128,896]{2,1,0:T(8,128)}, u32[]{:S(2)}, u32[]{:S(2)}) collective-permute-start(f32[2,128,896]{2,1,0:T(8,128)} %fusion.7), channel_id=1, source_target_pairs={{0,3},{1,0},{2,1},{3,2},{4,7},{5,4},{6,5},{7,6},{8,11},{9,8},{10,9... | collective-permute-start | bytes 2752520 | tf_op jit(solution)/shard_map/ppermute | solution.py:30
  110.5 19.2 %collective-permute-start.27 = (f32[2,128,896]{2,1,0:T(8,128)}, f32[2,128,896]{2,1,0:T(8,128)S(1)}, u32[]{:S(2)}, u32[]{:S(2)}) collective-permute-start(f32[2,128,896]{2,1,0:T(8,128)} %fusion.6), channel_id=1, source_target_pairs={{0,1},{1,2},{2,3},{3,0},{4,5},{5,6},{6,7},{7,4},{8,9},{9,10},{10,1... | collective-permute-start | bytes 2752520 | tf_op jit(solution)/shard_map/ppermute | solution.py:30
  111.6 18.0 %collective-permute-start.28 = (f32[2,128,896]{2,1,0:T(8,128)S(1)}, f32[2,128,896]{2,1,0:T(8,128)S(1)}, u32[]{:S(2)}, u32[]{:S(2)}) collective-permute-start(f32[2,128,896]{2,1,0:T(8,128)S(1)} %fusion.5), channel_id=1, source_target_pairs={{0,3},{1,0},{2,1},{3,2},{4,7},{5,4},{6,5},{7,6},{8,11},{9,8},{10,9... | collective-permute-start | bytes 2752520 | tf_op jit(solution)/shard_map/ppermute | solution.py:30
  132.9 16.3 %collective-permute-start.41 = (f32[144,640]{1,0:T(8,128)S(1)}, f32[144,640]{1,0:T(8,128)S(1)}, u32[]{:S(2)}, u32[]{:S(2)}) collective-permute-start(f32[144,640]{1,0:T(8,128)S(1)} %get-tuple-element.171), channel_id=1, source_target_pairs={{0,8},{8,0},{1,9},{9,1},{2,10},{10,2},{3,11},{11,3},{4,12},{12,4},... | collective-permute-start | bytes 1105928 | tf_op jit(solution)/shard_map/ppermute | solution.py:30
  147.8 21.7 %collective-permute-start.35 = (f32[2,64,896]{2,1,0:T(8,128)S(1)}, f32[2,64,896]{2,1,0:T(8,128)S(1)}, u32[]{:S(2)}, u32[]{:S(2)}) collective-permute-start(f32[2,64,896]{2,1,0:T(8,128)S(1)} %get-tuple-element.162), channel_id=1, source_target_pairs={{0,4},{4,0},{1,5},{5,1},{2,6},{6,2},{3,7},{7,3},{8,12},{12,8},{9,1... | collective-permute-start | bytes 1376264 | tf_op jit(solution)/shard_map/ppermute | solution.py:30
  149.1 19.4 %collective-permute-start.48 = (bf16[2,64,896]{2,1,0:T(8,128)(2,1)S(1)}, bf16[2,64,896]{2,1,0:T(8,128)(2,1)S(1)}, u32[]{:S(2)}, u32[]{:S(2)}) collective-permute-start(bf16[2,64,896]{2,1,0:T(8,128)(2,1)S(1)} %add_convert_fusion), channel_id=1, source_target_pairs={{0,1},{1,2},{2,3},{3,0},{4,5},{5,6},{6,7},{7,4},{8,9},{9,10},{10,1... | collective-permute-start | bytes 688136 | tf_op jit(solution)/shard_map/ppermute | solution.py:30
  149.9 14.6 %collective-permute-start.42 = (bf16[144,640]{1,0:T(8,128)(2,1)S(1)}, bf16[144,640]{1,0:T(8,128)(2,1)S(1)}, u32[]{:S(2)}, u32[]{:S(2)}) collective-permute-start(bf16[144,640]{1,0:T(8,128)(2,1)S(1)} %get-tuple-element.198), channel_id=1, source_target_pairs={{0,64},{64,0},{1,65},{65,1},{2,66},{66,2},{3,67},{67,3},{4,68},{68... | collective-permute-start | bytes 552968 | tf_op jit(solution)/shard_map/ppermute | solution.py:30
  169.5 19.0 %collective-permute-start.45 = (bf16[2,144,640]{2,1,0:T(8,128)(2,1)S(1)}, bf16[2,144,640]{2,1,0:T(8,128)(2,1)S(1)}, u32[]{:S(2)}, u32[]{:S(2)}) collective-permute-start(bf16[2,144,640]{2,1,0:T(8,128)(2,1)S(1)} %pad_maximum_fusion.4.refs_2_.refs_4_), channel_id=1, source_target_pairs={{0,16},{16,32},{32,48},{48,0},{1,17},{17,33},{33,49},{49,1},{2,18}... | collective-permute-start | bytes 1105928 | tf_op jit(solution)/shard_map/ppermute | solution.py:30
  190.5 22.6 %collective-permute-start.53 = (bf16[2,896,640]{2,1,0:T(8,128)(2,1)S(1)}, bf16[2,896,640]{2,1,0:T(8,128)(2,1)}, u32[]{:S(2)}, u32[]{:S(2)}) collective-permute-start(bf16[2,896,640]{2,1,0:T(8,128)(2,1)S(1)} %pad_maximum_fusion.refs_6_.refs_8_), channel_id=1, source_target_pairs={{0,8},{8,0},{1,9},{9,1},{2,10},{10,2},{3,11},{11,3},{4,12},{12,4},... | collective-permute-start | bytes 6881288 | tf_op jit(solution)/shard_map/ppermute | solution.py:30
  191.1 22.0 %collective-permute-start.52 = (bf16[4,2,64,896]{3,2,1,0:T(8,128)(2,1)S(1)}, bf16[4,2,64,896]{3,2,1,0:T(8,128)(2,1)}, u32[]{:S(2)}, u32[]{:S(2)}) collective-permute-start(bf16[4,2,64,896]{3,2,1,0:T(8,128)(2,1)S(1)} %pad_maximum_fusion.1.refs_0_), channel_id=1, source_target_pairs={{0,4},{4,0},{1,5},{5,1},{2,6},{6,2},{3,7},{7,3},{8,12},{12,8},{9,1... | collective-permute-start | bytes 2752520 | tf_op jit(solution)/shard_map/ppermute | solution.py:30
  192.6 29.9 %collective-permute-start.49 = (bf16[2,2,64,896]{3,2,1,0:T(8,128)(2,1)}, bf16[2,2,64,896]{3,2,1,0:T(8,128)(2,1)}, u32[]{:S(2)}, u32[]{:S(2)}) collective-permute-start(bf16[2,2,64,896]{3,2,1,0:T(8,128)(2,1)} %pad_maximum_fusion.3.refs_0_), channel_id=1, source_target_pairs={{0,3},{1,0},{2,1},{3,2},{4,7},{5,4},{6,5},{7,6},{8,11},{9,8},{10,9... | collective-permute-start | bytes 1376264 | tf_op jit(solution)/shard_map/ppermute | solution.py:30
  192.9 29.5 %collective-permute-start.50 = (bf16[2,2,64,896]{3,2,1,0:T(8,128)(2,1)}, bf16[2,2,64,896]{3,2,1,0:T(8,128)(2,1)}, u32[]{:S(2)}, u32[]{:S(2)}) collective-permute-start(bf16[2,2,64,896]{3,2,1,0:T(8,128)(2,1)} %pad_maximum_fusion.3.refs_0_), channel_id=1, source_target_pairs={{0,2},{1,3},{2,0},{3,1},{4,6},{5,7},{6,4},{7,5},{8,10},{9,11},{10,... | collective-permute-start | bytes 1376264 | tf_op jit(solution)/shard_map/ppermute | solution.py:30
  193.0 29.5 %collective-permute-start.51 = (bf16[2,2,64,896]{3,2,1,0:T(8,128)(2,1)}, bf16[2,2,64,896]{3,2,1,0:T(8,128)(2,1)}, u32[]{:S(2)}, u32[]{:S(2)}) collective-permute-start(bf16[2,2,64,896]{3,2,1,0:T(8,128)(2,1)} %pad_maximum_fusion.3.refs_0_), channel_id=1, source_target_pairs={{0,1},{1,2},{2,3},{3,0},{4,5},{5,6},{6,7},{7,4},{8,9},{9,10},{10,1... | collective-permute-start | bytes 1376264 | tf_op jit(solution)/shard_map/ppermute | solution.py:30
  234.2 14.9 %all-to-all-start = ((f32[128,2,128]{2,1,0:T(2,128)}), f32[128,2,128]{2,1,0:T(2,128)S(1)}, u32[]{:S(2)}, u32[]{:S(2)}) async-start(f32[128,2,128]{2,1,0:T(2,128)} %bitcast.83), calls=%async_computation | async-start | bytes 262144 | tf_op jit(solution)/shard_map/all_to_all | solution.py:357
  (68 other events, 691.7 us)

commit v5 on v4

--- a/solution.py
+++ b/solution.py
@@ -52,7 +52,7 @@
         out_shape=jax.ShapeDtypeStruct(blocks.shape, blocks.dtype),
         in_specs=[SMEM, VMEM],
         out_specs=VMEM,
-        compiler_params=params(6),
+        compiler_params=params(2),
         name="pick",
     )(order, blocks)
 
@@ -104,7 +104,7 @@
         out_shape=(pair, pair, pair, single, single, query),
         in_specs=[VMEM] * 6,
         out_specs=(VMEM,) * 6,
-        compiler_params=params(24),
+        compiler_params=params(18),
         cost_estimate=pl.CostEstimate(
             flops=2 * 576 * 1728 * 1728, bytes_accessed=12 * 1024 * 1024, transcendentals=0
         ),
@@ -128,7 +128,7 @@
         out_shape=(part, part),
         in_specs=[VMEM] * 3,
         out_specs=(VMEM, VMEM),
-        compiler_params=params(10),
+        compiler_params=params(6),
         cost_estimate=pl.CostEstimate(
             flops=4 * 64 * 864, bytes_accessed=2 * 1024 * 1024, transcendentals=0
         ),
@@ -193,7 +193,7 @@
         out_shape=(part, part),
         in_specs=[SMEM] + [VMEM] * 9,
         out_specs=(VMEM, VMEM),
-        compiler_params=params(12),
+        compiler_params=params(9),
         cost_estimate=pl.CostEstimate(
             flops=2 * 288 * 2560 * 640, bytes_accessed=6 * 1024 * 1024, transcendentals=0
         ),

time: 251 us -> 251 us (level)
  no operation moved by 1% of the time
where the time goes in v5:
time: 251 us; the launch traced here: 250 us
  waiting for transfers between devices  111 us (44%)
  starting transfers between devices  74.4 us (30%)
  Pallas kernels  33 us (13%)
  local copies, waits for them, and re-layouts  17.2 us (7%)
  other arithmetic  11.2 us (4%)
    ppermute x54, waiting for transfers between devices, take(): lax.ppermute(x, axis, [(i, (i - step) % count) for i in range(count)])  102 us
    ppermute x54, starting transfers between devices, take(): lax.ppermute(x, axis, [(i, (i - step) % count) for i in range(count)])  69.5 us
    pallas_call x2, Pallas kernels, rotate(): pl.pallas_call(rotate_kernel, out_shape=(pair, pair, pair, single, single...  14.7 us
    unnamed x96, local copies, waits for them, and re-layouts  12.6 us
    pallas_call x2, Pallas kernels, score(): pl.pallas_call(score_kernel, out_shape=jax.ShapeDtypeStruct((GROUP * SEQL...  11 us
    all_to_all x1, waiting for transfers between devices, per_device(): lax.all_to_all(spread.reshape(128, QUERIES, SEQLEN), AXES, 0, 0, tiled=True)  9.28 us
  transfers between devices with their start and end apart: 55, of which 20 were waited for; matrix products, arithmetic and copies ran while one was open for 5% of the time, Pallas kernels for 9%

profile of v5, /device:TPU:1, one launch (start us, length us, event | category | flops | bytes accessed | tf_op | source)
XLA Modules:
  0.0 250.5 jit_solution(1215319386992470643)
XLA Ops:
  10.9 3.9 %collective-permute-start.7 = (bf16[288,320]{1,0:T(8,128)(2,1)S(1)}, bf16[288,320]{1,0:T(8,128)(2,1)S(1)}, u32[]{:S(2)}, u32[]{:S(2)}) collective-permute-start(bf16[288,320]{1,0:T(8,128)(2,1)S(1)} %get-tuple-element.196), channel_id=1, source_target_pairs={{0,3},{1,0},{2,1},{3,2},{4,7},{5,4},{6,5},{7,6},{8,11},{9,8},{10,9... | collective-permute-start | bytes 552968 | tf_op jit(solution)/shard_map/ppermute | solution.py:30
  21.5 6.4 %collective-permute-done.8 = bf16[288,320]{1,0:T(8,128)(2,1)S(1)} collective-permute-done((bf16[288,320]{1,0:T(8,128)(2,1)S(1)}, bf16[288,320]{1,0:T(8,128)(2,1)S(1)}, u32[]{:S(2)}, u32[]{:S(2)}) %collective-permute-start.8) | collective-permute-done | bytes 184352 | tf_op jit(solution)/shard_map/ppermute | solution.py:30
  28.3 5.9 %collective-permute-done.9 = bf16[288,320]{1,0:T(8,128)(2,1)S(1)} collective-permute-done((bf16[288,320]{1,0:T(8,128)(2,1)S(1)}, bf16[288,320]{1,0:T(8,128)(2,1)S(1)}, u32[]{:S(2)}, u32[]{:S(2)}) %collective-permute-start.9) | collective-permute-done | bytes 184352 | tf_op jit(solution)/shard_map/ppermute | solution.py:30
  38.0 7.6 %rotate.2 = (f32[2,128,896]{2,1,0:T(8,128)S(1)}, f32[2,128,896]{2,1,0:T(8,128)}, f32[2,128,896]{2,1,0:T(8,128)}, f32[128,896]{1,0:T(8,128)S(1)}, f32[128,896]{1,0:T(8,128)S(1)}, /*index=5*/f32[4,16,896]{2,1,0:T(8,128)S(1)}) custom-call(bf16[144,1792]{1,0:T(8,128)(2,1)S(1)} %fusion.4.g0, bf16[144,1792]{1,0:T(8,128)(2,1)S(1)} %collective-permute-done.1.g1, ...), custom_call_target="tpu_custom_call" | custom-call | flops 3439853568 | bytes 12582912 | tf_op jit(solution)/shard_map/rotate/pallas_call | solution.py:102
  49.0 5.7 %collective-permute-done.10 = f32[128,896]{1,0:T(8,128)S(1)} collective-permute-done((f32[128,896]{1,0:T(8,128)S(1)}, f32[128,896]{1,0:T(8,128)S(1)}, u32[]{:S(2)}, u32[]{:S(2)}) %collective-permute-start.10) | collective-permute-done | bytes 458784 | tf_op jit(solution)/shard_map/ppermute | solution.py:30
  58.1 4.0 %collective-permute-start.17 = (bf16[320,640]{1,0:T(8,128)(2,1)}, bf16[320,640]{1,0:T(8,128)(2,1)}, u32[]{:S(2)}, u32[]{:S(2)}) collective-permute-start(bf16[320,640]{1,0:T(8,128)(2,1)} %refs_0_), channel_id=1, source_target_pairs={{0,64},{64,0},{1,65},{65,1},{2,66},{66,2},{3,67},{67,3},{4,68},{68... | collective-permute-start | bytes 1228808 | tf_op jit(solution)/shard_map/ppermute | solution.py:30
  69.2 7.1 %rotate.3 = (f32[2,128,896]{2,1,0:T(8,128)S(1)}, f32[2,128,896]{2,1,0:T(8,128)S(1)}, f32[2,128,896]{2,1,0:T(8,128)S(1)}, f32[128,896]{1,0:T(8,128)}, f32[128,896]{1,0:T(8,128)}, /*index=5*/f32[4,16,896]{2,1,0:T(8,128)S(1)}) custom-call(bf16[144,1792]{1,0:T(8,128)(2,1)S(1)} %collective-permute-done.20.g0, bf16[144,1792]{1,0:T(8,128)(2,1)S(1)} %collective-permute-done.13.g1, ...), custom_call_target="tpu_custom_call" | custom-call | flops 3439853568 | bytes 12582912 | tf_op jit(solution)/shard_map/rotate/pallas_call | solution.py:102
  78.1 7.9 %collective-permute-done.23 = f32[2,16,896]{2,1,0:T(8,128)S(1)} collective-permute-done((f32[2,16,896]{2,1,0:T(8,128)S(1)}, f32[2,16,896]{2,1,0:T(8,128)S(1)}, u32[]{:S(2)}, u32[]{:S(2)}) %collective-permute-start.23) | collective-permute-done | bytes 114720 | tf_op jit(solution)/shard_map/ppermute | solution.py:30
  86.0 5.3 %collective-permute-done.24 = f32[2,16,896]{2,1,0:T(8,128)S(1)} collective-permute-done((f32[2,16,896]{2,1,0:T(8,128)S(1)}, f32[2,16,896]{2,1,0:T(8,128)S(1)}, u32[]{:S(2)}, u32[]{:S(2)}) %collective-permute-start.24) | collective-permute-done | bytes 114720 | tf_op jit(solution)/shard_map/ppermute | solution.py:30
  91.6 4.4 %collective-permute-done.25 = f32[2,16,896]{2,1,0:T(8,128)S(1)} collective-permute-done((f32[2,16,896]{2,1,0:T(8,128)S(1)}, f32[2,16,896]{2,1,0:T(8,128)S(1)}, u32[]{:S(2)}, u32[]{:S(2)}) %collective-permute-start.25) | collective-permute-done | bytes 114720 | tf_op jit(solution)/shard_map/ppermute | solution.py:30
  99.0 8.0 %collective-permute-done.19.refs_3_ = bf16[320,640]{1,0:T(8,128)(2,1)S(1)} collective-permute-done((bf16[320,640]{1,0:T(8,128)(2,1)}, bf16[320,640]{1,0:T(8,128)(2,1)S(1)}, u32[]{:S(2)}, u32[]{:S(2)}) %collective-permute-start.19) | collective-permute-done | bytes 409632 | tf_op jit(solution)/shard_map/ppermute | solution.py:30
  120.3 6.8 %collective-permute-done.32.refs_2_ = bf16[320,640]{1,0:T(8,128)(2,1)S(1)} collective-permute-done((bf16[320,640]{1,0:T(8,128)(2,1)}, bf16[320,640]{1,0:T(8,128)(2,1)S(1)}, u32[]{:S(2)}, u32[]{:S(2)}) %collective-permute-start.32) | collective-permute-done | bytes 409632 | tf_op jit(solution)/shard_map/ppermute | solution.py:30
  129.7 3.2 %rotate_acts.1 = (f32[144,640]{1,0:T(8,128)S(1)}, f32[144,640]{1,0:T(8,128)S(1)}) custom-call(s32[8]{0:T(128)S(1)} %stack.193.order, bf16[8,288,320]{2,1,0:T(8,128)(2,1)S(1)} %constant_dynamic-update-slice_fusion.acts, bf16[320,640]{1,0:T(8,128)(2,1)} %refs_0_, bf16[320,640]{1,0:T(8,128)(2,1)} %collective-permute-done.18.refs_1_, ...), custom_call_target="tpu_custom_call" | custom-call | flops 943718400 | bytes 6291456 | tf_op jit(solution)/shard_map/rotate_acts/pallas_call | solution.py:191
  132.9 14.8 %collective-permute-start.41 = (f32[144,640]{1,0:T(8,128)S(1)}, f32[144,640]{1,0:T(8,128)S(1)}, u32[]{:S(2)}, u32[]{:S(2)}) collective-permute-start(f32[144,640]{1,0:T(8,128)S(1)} %get-tuple-element.171), channel_id=1, source_target_pairs={{0,8},{8,0},{1,9},{9,1},{2,10},{10,2},{3,11},{11,3},{4,12},{12,4},... | collective-permute-start | bytes 1105928 | tf_op jit(solution)/shard_map/ppermute | solution.py:30
  154.5 10.0 %collective-permute-done.42 = bf16[144,640]{1,0:T(8,128)(2,1)S(1)} collective-permute-done((bf16[144,640]{1,0:T(8,128)(2,1)S(1)}, bf16[144,640]{1,0:T(8,128)(2,1)S(1)}, u32[]{:S(2)}, u32[]{:S(2)}) %collective-permute-start.42) | collective-permute-done | bytes 184352 | tf_op jit(solution)/shard_map/ppermute | solution.py:30
  165.2 3.3 %collective-permute-start.46 = (bf16[2,64,896]{2,1,0:T(8,128)(2,1)S(1)}, bf16[2,64,896]{2,1,0:T(8,128)(2,1)S(1)}, u32[]{:S(2)}, u32[]{:S(2)}) collective-permute-start(bf16[2,64,896]{2,1,0:T(8,128)(2,1)S(1)} %add_convert_fusion), channel_id=1, source_target_pairs={{0,3},{1,0},{2,1},{3,2},{4,7},{5,4},{6,5},{7,6},{8,11},{9,8},{10,9... | collective-permute-start | bytes 688136 | tf_op jit(solution)/shard_map/ppermute | solution.py:30
  173.3 3.2 %collective-permute-done.46 = bf16[2,64,896]{2,1,0:T(8,128)(2,1)S(1)} collective-permute-done((bf16[2,64,896]{2,1,0:T(8,128)(2,1)S(1)}, bf16[2,64,896]{2,1,0:T(8,128)(2,1)S(1)}, u32[]{:S(2)}, u32[]{:S(2)}) %collective-permute-start.46) | collective-permute-done | bytes 229408 | tf_op jit(solution)/shard_map/ppermute | solution.py:30
  177.1 4.6 %collective-permute-done.40 = bf16[4,16,896]{2,1,0:T(8,128)(2,1)S(1)} collective-permute-done((bf16[4,16,896]{2,1,0:T(8,128)(2,1)S(1)}, bf16[4,16,896]{2,1,0:T(8,128)(2,1)S(1)}, u32[]{:S(2)}, u32[]{:S(2)}) %collective-permute-start.40) | collective-permute-done | bytes 114720 | tf_op jit(solution)/shard_map/ppermute | solution.py:30
  181.8 6.7 %collective-permute-done.45.refs_5_.refs_7_ = bf16[2,144,640]{2,1,0:T(8,128)(2,1)S(1)} collective-permute-done((bf16[2,144,640]{2,1,0:T(8,128)(2,1)S(1)}, bf16[2,144,640]{2,1,0:T(8,128)(2,1)S(1)}, u32[]{:S(2)}, u32[]{:S(2)}) %collective-permute-start.45) | collective-permute-done | bytes 368672 | tf_op jit(solution)/shard_map/ppermute | solution.py:30
  194.0 19.1 %collective-permute-done.52.refs_1_ = bf16[4,2,64,896]{3,2,1,0:T(8,128)(2,1)} collective-permute-done((bf16[4,2,64,896]{3,2,1,0:T(8,128)(2,1)S(1)}, bf16[4,2,64,896]{3,2,1,0:T(8,128)(2,1)}, u32[]{:S(2)}, u32[]{:S(2)}) %collective-permute-start.52) | collective-permute-done | bytes 917536 | tf_op jit(solution)/shard_map/ppermute | solution.py:30
  217.0 5.4 %score.2 = f32[512,2]{1,0:T(8,128)S(1)} custom-call(bf16[4,2,64,896]{3,2,1,0:T(8,128)(2,1)S(1)} %pad_maximum_fusion.1.refs_0_, bf16[4,2,64,896]{3,2,1,0:T(8,128)(2,1)} %collective-permute-done.52.refs_1_, bf16[2,144,640]{2,1,0:T(8,128)(2,1)S(1)} %copy-done.6, bf16[2,144,640]{2,1,0:T(8,128)(2,1)S(1)} %copy-done.12, bf16[2,144,640]{2,1,0:T(8,128)(2,1)S(1)} %copy-done.15, ...), custom_call_target="tpu_custom_call" | custom-call | flops 2264924160 | bytes 8388608 | tf_op jit(solution)/shard_map/score/pallas_call | solution.py:165
  226.7 5.6 %score.3 = f32[512,2]{1,0:T(8,128)S(1)} custom-call(bf16[2,2,64,896]{3,2,1,0:T(8,128)(2,1)} %pad_maximum_fusion.3.refs_0_, bf16[2,2,64,896]{3,2,1,0:T(8,128)(2,1)} %collective-permute-done.49.refs_1_, bf16[2,2,64,896]{3,2,1,0:T(8,128)(2,1)} %collective-permute-done.50.refs_2_, bf16[2,2,64,896]{3,2,1,0:T(8,128)(2,1)} %collective-permute-done.51.refs_3_, ...), custom_call_target="tpu_custom_call" | custom-call | flops 2264924160 | bytes 8388608 | tf_op jit(solution)/shard_map/score/pallas_call | solution.py:165
  234.2 4.9 %all-to-all-start = ((f32[128,2,128]{2,1,0:T(2,128)}), f32[128,2,128]{2,1,0:T(2,128)S(1)}, u32[]{:S(2)}, u32[]{:S(2)}) async-start(f32[128,2,128]{2,1,0:T(2,128)} %bitcast.83), calls=%async_computation | async-start | bytes 262144 | tf_op jit(solution)/shard_map/all_to_all | solution.py:357
  239.8 9.3 %all-to-all-done = f32[128,2,128]{2,1,0:T(2,128)S(1)} async-done(((f32[128,2,128]{2,1,0:T(2,128)}), f32[128,2,128]{2,1,0:T(2,128)S(1)}, u32[]{:S(2)}, u32[]{:S(2)}) %all-to-all-start) | async-done | bytes 131104 | tf_op jit(solution)/shard_map/all_to_all | solution.py:357
  (249 shorter events, 85.2 us)
Async XLA Ops:
  2.8 31.4 %collective-permute-start.4 = (bf16[1792,896]{1,0:T(8,128)(2,1)S(1)}, bf16[1792,896]{1,0:T(8,128)(2,1)}, u32[]{:S(2)}, u32[]{:S(2)}) collective-permute-start(bf16[1792,896]{1,0:T(8,128)(2,1)S(1)} %pad.21.own_basis), channel_id=1, source_target_pairs={{0,8},{8,0},{1,9},{9,1},{2,10},{10,2},{3,11},{11,3},{4,12},{12,4},... | collective-permute-start | bytes 9633800 | tf_op jit(solution)/shard_map/ppermute | solution.py:30
  14.8 19.4 %collective-permute-start.1 = (bf16[144,1792]{1,0:T(8,128)(2,1)S(1)}, bf16[144,1792]{1,0:T(8,128)(2,1)S(1)}, u32[]{:S(2)}, u32[]{:S(2)}) collective-permute-start(bf16[144,1792]{1,0:T(8,128)(2,1)S(1)} %fusion.4.g0), channel_id=1, source_target_pairs={{0,64},{64,0},{1,65},{65,1},{2,66},{66,2},{3,67},{67,3},{4,68},{68... | collective-permute-start | bytes 1548296 | tf_op jit(solution)/shard_map/ppermute | solution.py:30
  17.6 16.6 %collective-permute-start.2 = (bf16[144,1792]{1,0:T(8,128)(2,1)S(1)}, bf16[144,1792]{1,0:T(8,128)(2,1)S(1)}, u32[]{:S(2)}, u32[]{:S(2)}) collective-permute-start(bf16[144,1792]{1,0:T(8,128)(2,1)S(1)} %fusion.4.g0), channel_id=1, source_target_pairs={{0,48},{16,0},{32,16},{48,32},{1,49},{17,1},{33,17},{49,33},{2,50}... | collective-permute-start | bytes 1548296 | tf_op jit(solution)/shard_map/ppermute | solution.py:30
  34.2 14.0 %collective-permute-start.13 = (bf16[144,1792]{1,0:T(8,128)(2,1)S(1)}, bf16[144,1792]{1,0:T(8,128)(2,1)S(1)}, u32[]{:S(2)}, u32[]{:S(2)}) collective-permute-start(bf16[144,1792]{1,0:T(8,128)(2,1)S(1)} %collective-permute-done.1.g1), channel_id=1, source_target_pairs={{0,16},{16,32},{32,48},{48,0},{1,17},{17,33},{33,49},{49,1},{2,18}... | collective-permute-start | bytes 1548296 | tf_op jit(solution)/shard_map/ppermute | solution.py:30
  35.6 30.9 %collective-permute-start.20 = (bf16[144,1792]{1,0:T(8,128)(2,1)S(1)}, bf16[144,1792]{1,0:T(8,128)(2,1)S(1)}, u32[]{:S(2)}, u32[]{:S(2)}) collective-permute-start(bf16[144,1792]{1,0:T(8,128)(2,1)S(1)} %collective-permute-done.1.g1), channel_id=1, source_target_pairs={{0,48},{16,0},{32,16},{48,32},{1,49},{17,1},{33,17},{49,33},{2,50}... | collective-permute-start | bytes 1548296 | tf_op jit(solution)/shard_map/ppermute | solution.py:30
  37.0 20.2 %collective-permute-start.12 = (bf16[144,1792]{1,0:T(8,128)(2,1)S(1)}, bf16[144,1792]{1,0:T(8,128)(2,1)S(1)}, u32[]{:S(2)}, u32[]{:S(2)}) collective-permute-start(bf16[144,1792]{1,0:T(8,128)(2,1)S(1)} %collective-permute-done.2.g2), channel_id=1, source_target_pairs={{0,48},{16,0},{32,16},{48,32},{1,49},{17,1},{33,17},{49,33},{2,50}... | collective-permute-start | bytes 1548296 | tf_op jit(solution)/shard_map/ppermute | solution.py:30
  54.7 23.2 %collective-permute-start.26 = (bf16[4,288,320]{2,1,0:T(8,128)(2,1)S(1)}, bf16[4,288,320]{2,1,0:T(8,128)(2,1)S(1)}, u32[]{:S(2)}, u32[]{:S(2)}) collective-permute-start(bf16[4,288,320]{2,1,0:T(8,128)(2,1)S(1)} %pad_maximum_fusion.2), channel_id=1, source_target_pairs={{0,4},{4,0},{1,5},{5,1},{2,6},{6,2},{3,7},{7,3},{8,12},{12,8},{9,1... | collective-permute-start | bytes 2211848 | tf_op jit(solution)/shard_map/ppermute | solution.py:30
  58.1 37.9 %collective-permute-start.17 = (bf16[320,640]{1,0:T(8,128)(2,1)}, bf16[320,640]{1,0:T(8,128)(2,1)}, u32[]{:S(2)}, u32[]{:S(2)}) collective-permute-start(bf16[320,640]{1,0:T(8,128)(2,1)} %refs_0_), channel_id=1, source_target_pairs={{0,64},{64,0},{1,65},{65,1},{2,66},{66,2},{3,67},{67,3},{4,68},{68... | collective-permute-start | bytes 1228808 | tf_op jit(solution)/shard_map/ppermute | solution.py:30
  62.1 36.6 %collective-permute-start.18 = (bf16[320,640]{1,0:T(8,128)(2,1)}, bf16[320,640]{1,0:T(8,128)(2,1)}, u32[]{:S(2)}, u32[]{:S(2)}) collective-permute-start(bf16[320,640]{1,0:T(8,128)(2,1)} %refs_0_), channel_id=1, source_target_pairs={{0,48},{16,0},{32,16},{48,32},{1,49},{17,1},{33,17},{49,33},{2,50}... | collective-permute-start | bytes 1228808 | tf_op jit(solution)/shard_map/ppermute | solution.py:30
  64.6 42.4 %collective-permute-start.15 = (f32[2,128,896]{2,1,0:T(8,128)}, f32[2,128,896]{2,1,0:T(8,128)}, u32[]{:S(2)}, u32[]{:S(2)}) collective-permute-start(f32[2,128,896]{2,1,0:T(8,128)} %fusion.8), channel_id=1, source_target_pairs={{0,1},{1,2},{2,3},{3,0},{4,5},{5,6},{6,7},{7,4},{8,9},{9,10},{10,1... | collective-permute-start | bytes 2752520 | tf_op jit(solution)/shard_map/ppermute | solution.py:30
  66.5 40.5 %collective-permute-start.16 = (f32[2,128,896]{2,1,0:T(8,128)}, f32[2,128,896]{2,1,0:T(8,128)}, u32[]{:S(2)}, u32[]{:S(2)}) collective-permute-start(f32[2,128,896]{2,1,0:T(8,128)} %fusion.7), channel_id=1, source_target_pairs={{0,3},{1,0},{2,1},{3,2},{4,7},{5,4},{6,5},{7,6},{8,11},{9,8},{10,9... | collective-permute-start | bytes 2752520 | tf_op jit(solution)/shard_map/ppermute | solution.py:30
  110.5 19.2 %collective-permute-start.27 = (f32[2,128,896]{2,1,0:T(8,128)}, f32[2,128,896]{2,1,0:T(8,128)S(1)}, u32[]{:S(2)}, u32[]{:S(2)}) collective-permute-start(f32[2,128,896]{2,1,0:T(8,128)} %fusion.6), channel_id=1, source_target_pairs={{0,1},{1,2},{2,3},{3,0},{4,5},{5,6},{6,7},{7,4},{8,9},{9,10},{10,1... | collective-permute-start | bytes 2752520 | tf_op jit(solution)/shard_map/ppermute | solution.py:30
  111.6 18.0 %collective-permute-start.28 = (f32[2,128,896]{2,1,0:T(8,128)S(1)}, f32[2,128,896]{2,1,0:T(8,128)S(1)}, u32[]{:S(2)}, u32[]{:S(2)}) collective-permute-start(f32[2,128,896]{2,1,0:T(8,128)S(1)} %fusion.5), channel_id=1, source_target_pairs={{0,3},{1,0},{2,1},{3,2},{4,7},{5,4},{6,5},{7,6},{8,11},{9,8},{10,9... | collective-permute-start | bytes 2752520 | tf_op jit(solution)/shard_map/ppermute | solution.py:30
  132.9 16.3 %collective-permute-start.41 = (f32[144,640]{1,0:T(8,128)S(1)}, f32[144,640]{1,0:T(8,128)S(1)}, u32[]{:S(2)}, u32[]{:S(2)}) collective-permute-start(f32[144,640]{1,0:T(8,128)S(1)} %get-tuple-element.171), channel_id=1, source_target_pairs={{0,8},{8,0},{1,9},{9,1},{2,10},{10,2},{3,11},{11,3},{4,12},{12,4},... | collective-permute-start | bytes 1105928 | tf_op jit(solution)/shard_map/ppermute | solution.py:30
  147.8 21.7 %collective-permute-start.35 = (f32[2,64,896]{2,1,0:T(8,128)S(1)}, f32[2,64,896]{2,1,0:T(8,128)S(1)}, u32[]{:S(2)}, u32[]{:S(2)}) collective-permute-start(f32[2,64,896]{2,1,0:T(8,128)S(1)} %get-tuple-element.162), channel_id=1, source_target_pairs={{0,4},{4,0},{1,5},{5,1},{2,6},{6,2},{3,7},{7,3},{8,12},{12,8},{9,1... | collective-permute-start | bytes 1376264 | tf_op jit(solution)/shard_map/ppermute | solution.py:30
  149.1 19.4 %collective-permute-start.48 = (bf16[2,64,896]{2,1,0:T(8,128)(2,1)S(1)}, bf16[2,64,896]{2,1,0:T(8,128)(2,1)S(1)}, u32[]{:S(2)}, u32[]{:S(2)}) collective-permute-start(bf16[2,64,896]{2,1,0:T(8,128)(2,1)S(1)} %add_convert_fusion), channel_id=1, source_target_pairs={{0,1},{1,2},{2,3},{3,0},{4,5},{5,6},{6,7},{7,4},{8,9},{9,10},{10,1... | collective-permute-start | bytes 688136 | tf_op jit(solution)/shard_map/ppermute | solution.py:30
  149.9 14.6 %collective-permute-start.42 = (bf16[144,640]{1,0:T(8,128)(2,1)S(1)}, bf16[144,640]{1,0:T(8,128)(2,1)S(1)}, u32[]{:S(2)}, u32[]{:S(2)}) collective-permute-start(bf16[144,640]{1,0:T(8,128)(2,1)S(1)} %get-tuple-element.198), channel_id=1, source_target_pairs={{0,64},{64,0},{1,65},{65,1},{2,66},{66,2},{3,67},{67,3},{4,68},{68... | collective-permute-start | bytes 552968 | tf_op jit(solution)/shard_map/ppermute | solution.py:30
  169.5 19.0 %collective-permute-start.45 = (bf16[2,144,640]{2,1,0:T(8,128)(2,1)S(1)}, bf16[2,144,640]{2,1,0:T(8,128)(2,1)S(1)}, u32[]{:S(2)}, u32[]{:S(2)}) collective-permute-start(bf16[2,144,640]{2,1,0:T(8,128)(2,1)S(1)} %pad_maximum_fusion.4.refs_2_.refs_4_), channel_id=1, source_target_pairs={{0,16},{16,32},{32,48},{48,0},{1,17},{17,33},{33,49},{49,1},{2,18}... | collective-permute-start | bytes 1105928 | tf_op jit(solution)/shard_map/ppermute | solution.py:30
  190.5 22.6 %collective-permute-start.53 = (bf16[2,896,640]{2,1,0:T(8,128)(2,1)S(1)}, bf16[2,896,640]{2,1,0:T(8,128)(2,1)}, u32[]{:S(2)}, u32[]{:S(2)}) collective-permute-start(bf16[2,896,640]{2,1,0:T(8,128)(2,1)S(1)} %pad_maximum_fusion.refs_6_.refs_8_), channel_id=1, source_target_pairs={{0,8},{8,0},{1,9},{9,1},{2,10},{10,2},{3,11},{11,3},{4,12},{12,4},... | collective-permute-start | bytes 6881288 | tf_op jit(solution)/shard_map/ppermute | solution.py:30
  191.1 22.0 %collective-permute-start.52 = (bf16[4,2,64,896]{3,2,1,0:T(8,128)(2,1)S(1)}, bf16[4,2,64,896]{3,2,1,0:T(8,128)(2,1)}, u32[]{:S(2)}, u32[]{:S(2)}) collective-permute-start(bf16[4,2,64,896]{3,2,1,0:T(8,128)(2,1)S(1)} %pad_maximum_fusion.1.refs_0_), channel_id=1, source_target_pairs={{0,4},{4,0},{1,5},{5,1},{2,6},{6,2},{3,7},{7,3},{8,12},{12,8},{9,1... | collective-permute-start | bytes 2752520 | tf_op jit(solution)/shard_map/ppermute | solution.py:30
  192.6 29.9 %collective-permute-start.49 = (bf16[2,2,64,896]{3,2,1,0:T(8,128)(2,1)}, bf16[2,2,64,896]{3,2,1,0:T(8,128)(2,1)}, u32[]{:S(2)}, u32[]{:S(2)}) collective-permute-start(bf16[2,2,64,896]{3,2,1,0:T(8,128)(2,1)} %pad_maximum_fusion.3.refs_0_), channel_id=1, source_target_pairs={{0,3},{1,0},{2,1},{3,2},{4,7},{5,4},{6,5},{7,6},{8,11},{9,8},{10,9... | collective-permute-start | bytes 1376264 | tf_op jit(solution)/shard_map/ppermute | solution.py:30
  192.9 29.5 %collective-permute-start.50 = (bf16[2,2,64,896]{3,2,1,0:T(8,128)(2,1)}, bf16[2,2,64,896]{3,2,1,0:T(8,128)(2,1)}, u32[]{:S(2)}, u32[]{:S(2)}) collective-permute-start(bf16[2,2,64,896]{3,2,1,0:T(8,128)(2,1)} %pad_maximum_fusion.3.refs_0_), channel_id=1, source_target_pairs={{0,2},{1,3},{2,0},{3,1},{4,6},{5,7},{6,4},{7,5},{8,10},{9,11},{10,... | collective-permute-start | bytes 1376264 | tf_op jit(solution)/shard_map/ppermute | solution.py:30
  193.0 29.5 %collective-permute-start.51 = (bf16[2,2,64,896]{3,2,1,0:T(8,128)(2,1)}, bf16[2,2,64,896]{3,2,1,0:T(8,128)(2,1)}, u32[]{:S(2)}, u32[]{:S(2)}) collective-permute-start(bf16[2,2,64,896]{3,2,1,0:T(8,128)(2,1)} %pad_maximum_fusion.3.refs_0_), channel_id=1, source_target_pairs={{0,1},{1,2},{2,3},{3,0},{4,5},{5,6},{6,7},{7,4},{8,9},{9,10},{10,1... | collective-permute-start | bytes 1376264 | tf_op jit(solution)/shard_map/ppermute | solution.py:30
  234.2 14.9 %all-to-all-start = ((f32[128,2,128]{2,1,0:T(2,128)}), f32[128,2,128]{2,1,0:T(2,128)S(1)}, u32[]{:S(2)}, u32[]{:S(2)}) async-start(f32[128,2,128]{2,1,0:T(2,128)} %bitcast.83), calls=%async_computation | async-start | bytes 262144 | tf_op jit(solution)/shard_map/all_to_all | solution.py:357
  (68 other events, 691.7 us)
